TPU v7x, 512 devices: a whole 4x4x16 slice. The times are simulated.
512 devices in a mesh: leaf: 16 (over z_hi, x, core), node: 32 (over y, z_lo).
Axes of the slice: x: 4, y: 4, z: 16 (z_hi: 2, z_lo: 8; z = z_hi * 8 + z_lo), core: 2. Of those that a mesh axis runs over, the one named last changes fastest.
Arguments:
- queries: bfloat16 [65536, 4096], P(('leaf', 'node')), parts along dimension 0, may hold values from -60 to 60
- key_states: bfloat16 [65536, 512], P(('leaf', 'node')), parts along dimension 0, may hold values from -4 to 4
- state_values: bfloat16 [65536, 512], P(('leaf', 'node')), parts along dimension 0, may hold values from -4 to 4
- out_grad: bfloat16 [65536, 4096], P(('leaf', 'node')), parts along dimension 0, may hold values from -4 to 4
- block_depth: int32 [512], P('leaf'), parts along dimension 0, may hold values from 0 to 3, as said below
Outputs:
- attended: bfloat16 [65536, 4096], P(('leaf', 'node')), parts along dimension 0
- query_grad: bfloat16 [65536, 4096], P(('leaf', 'node')), parts along dimension 0
- key_grad: bfloat16 [65536, 512], P(('leaf', 'node')), parts along dimension 0
- value_grad: bfloat16 [65536, 512], P(('leaf', 'node')), parts along dimension 0
There are 16 independent parts, one for each index of `leaf`. A program takes and returns all parts, laid end to end along the dimension named above; each array names one. Nothing has to cross between parts.
Inputs may be any that keep to these rules, and one draw needn't show every extreme that they name: block_depth[0] = 0; every later block has depth 1 to one more than the block before it; some block has depth 4 - 1.
All inputs are finite; a program needn't handle non-finite values.
Results may differ from a plain program's by a relative error of at most 0.035.
Values may be sent and summed in bfloat16 or wider, within the bound.
No kernel may reach another device: no remote copies, remote signals or barrier semaphores. Data moves between devices by JAX's collectives and lax.ppermute only.
A program may use at most 128 MiB of HBM per device.

v0:
```python
import jax
import jax.numpy as jnp
from jax import lax
from jax.sharding import PartitionSpec as P

HEAD_SIZE = 128
DEPTH = 4


def entering(array, axis, combine, identity):
    count, index = (lax.axis_size(axis), lax.axis_index(axis))
    everything = jax.tree.map(lambda part: lax.all_gather(part, axis), array)
    start = jax.tree.map(
        lambda part, zero: jnp.broadcast_to(jnp.asarray(zero, part.dtype), part.shape),
        array,
        identity,
    )

    def hop(k, before):
        at = count - 1 - k
        reached = at > index
        new = combine(before, jax.tree.map(lambda part: part[at], everything))
        return jax.tree.map(lambda a, b: jnp.where(reached, a, b), new, before)

    return lax.fori_loop(0, count, hop, start)


def ancestor_table(block_depth):
    block_count = block_depth.shape[0]
    block_ids = jnp.arange(block_count, dtype=jnp.int32)
    depth_levels = jnp.arange(DEPTH, dtype=jnp.int32)
    found_at = (block_depth[None, :, None] == depth_levels[None, None, :]) & (
        block_ids[None, :, None] <= block_ids[:, None, None]
    )
    latest = jnp.max(jnp.where(found_at, block_ids[None, :, None], -1), axis=1)
    slot_valid = depth_levels[None, :] <= block_depth[:, None]
    return (jnp.where(slot_valid, latest, 0), slot_valid)


def allowed_mask(own_depth, slot_valid, count_of_rows):
    depth_levels = jnp.arange(DEPTH, dtype=jnp.int32)
    positions = jnp.arange(count_of_rows, dtype=jnp.int32)
    causal = positions[None, :] <= positions[:, None]
    earlier = (depth_levels < own_depth)[None, :, None]
    same_block = (depth_levels == own_depth)[None, :, None] & causal[:, None, :]
    allowed = slot_valid[None, :, None] & (earlier | same_block)
    return allowed.reshape(count_of_rows, DEPTH * count_of_rows)


def head_group(query_cols, key_cols, value_cols, grad_cols, allowed):
    count_of_rows = query_cols.shape[0]
    head_width = key_cols.shape[1]
    group_members = query_cols.shape[1] // head_width
    score_scale = head_width ** (-0.5)
    heads_of_query = query_cols.reshape(count_of_rows, group_members, head_width)
    gradient_heads = grad_cols.reshape(count_of_rows, group_members, head_width)
    scores = (
        jnp.einsum("tjd,ud->jtu", heads_of_query, key_cols, preferred_element_type=jnp.float32)
        * score_scale
    )
    scores = jnp.where(allowed[None], scores, -jnp.inf)
    row_max = jnp.max(scores, axis=-1, keepdims=True)
    weights = jnp.exp(scores - row_max)
    softmax_probs = weights / jnp.sum(weights, axis=-1, keepdims=True)
    probs_low = softmax_probs.astype(jnp.bfloat16)
    attended = jnp.einsum(
        "jtu,ud->tjd", probs_low, value_cols, preferred_element_type=jnp.float32
    ).astype(jnp.bfloat16)
    row_delta = jnp.einsum(
        "tjd,tjd->jt", gradient_heads.astype(jnp.float32), attended.astype(jnp.float32)
    )
    dprobs = jnp.einsum(
        "tjd,ud->jtu", gradient_heads, value_cols, preferred_element_type=jnp.float32
    )
    dscores_low = (softmax_probs * (dprobs - row_delta[..., None])).astype(jnp.bfloat16)
    query_grad = (
        jnp.einsum("jtu,ud->tjd", dscores_low, key_cols, preferred_element_type=jnp.float32)
        * score_scale
    ).astype(jnp.bfloat16)
    key_portion = (
        jnp.einsum("jtu,tjd->ud", dscores_low, heads_of_query, preferred_element_type=jnp.float32)
        * score_scale
    )
    value_portion = jnp.einsum(
        "jtu,tjd->ud", probs_low, gradient_heads, preferred_element_type=jnp.float32
    )
    return (
        attended.reshape(count_of_rows, -1),
        query_grad.reshape(count_of_rows, -1),
        key_portion,
        value_portion,
    )


def local(queries, key_states, state_values, out_grad, block_depth):
    count_of_rows, feat_width = key_states.shape
    head_width = HEAD_SIZE
    kv_heads = feat_width // head_width
    group_width = queries.shape[1] // kv_heads
    upper_count = DEPTH - 1
    device_index = lax.axis_index("node")
    anc_table, slot_valid = ancestor_table(block_depth)
    path_slots = anc_table[device_index]
    path_valid = slot_valid[device_index]
    own_depth = block_depth[device_index]
    depth_levels = jnp.arange(DEPTH, dtype=jnp.int32)
    own_slot = depth_levels == own_depth
    every_key, every_value = (
        lax.all_gather(key_states, "node", axis=0, tiled=True),
        lax.all_gather(state_values, "node", axis=0, tiled=True),
    )
    block_count = every_key.shape[0] // count_of_rows
    key_path = jnp.take(
        every_key.reshape(block_count, count_of_rows, feat_width), path_slots, axis=0
    )
    value_path = jnp.take(
        every_value.reshape(block_count, count_of_rows, feat_width), path_slots, axis=0
    )
    key_path = key_path.reshape(DEPTH * count_of_rows, feat_width)
    value_path = value_path.reshape(DEPTH * count_of_rows, feat_width)
    allowed = allowed_mask(own_depth, path_valid, count_of_rows)

    def one_head(head_index, buffers):
        attended_all, qgrad_all, kgrad_all, vgrad_all = buffers
        query_cols = lax.dynamic_slice_in_dim(queries, head_index * group_width, group_width, 1)
        grad_cols = lax.dynamic_slice_in_dim(out_grad, head_index * group_width, group_width, 1)
        key_cols = lax.dynamic_slice_in_dim(key_path, head_index * head_width, head_width, 1)
        value_cols = lax.dynamic_slice_in_dim(value_path, head_index * head_width, head_width, 1)
        head_results = head_group(query_cols, key_cols, value_cols, grad_cols, allowed)
        attended_all = lax.dynamic_update_slice_in_dim(
            attended_all, head_results[0], head_index * group_width, 1
        )
        qgrad_all = lax.dynamic_update_slice_in_dim(
            qgrad_all, head_results[1], head_index * group_width, 1
        )
        kgrad_all = lax.dynamic_update_slice_in_dim(
            kgrad_all, head_results[2], head_index * head_width, 1
        )
        vgrad_all = lax.dynamic_update_slice_in_dim(
            vgrad_all, head_results[3], head_index * head_width, 1
        )
        return (attended_all, qgrad_all, kgrad_all, vgrad_all)

    start_buffers = (
        jnp.zeros(queries.shape, jnp.bfloat16),
        jnp.zeros(queries.shape, jnp.bfloat16),
        jnp.zeros((DEPTH * count_of_rows, feat_width), jnp.float32),
        jnp.zeros((DEPTH * count_of_rows, feat_width), jnp.float32),
    )
    attended, query_grad, kgrad_all, vgrad_all = lax.fori_loop(0, kv_heads, one_head, start_buffers)
    key_terms = kgrad_all.reshape(DEPTH, count_of_rows, feat_width)
    value_terms = vgrad_all.reshape(DEPTH, count_of_rows, feat_width)
    above_own = (depth_levels < own_depth)[:upper_count, None, None]
    send_key = jnp.where(above_own, key_terms[:upper_count], 0.0)
    send_value = jnp.where(above_own, value_terms[:upper_count], 0.0)
    upper_levels = jnp.arange(upper_count, dtype=jnp.float32)

    def accumulate(earlier_part, later_part):
        early_key, early_value, early_depth = earlier_part
        late_key, late_value, late_depth = later_part
        inside = (late_depth[0] > upper_levels)[:, None, None]
        return (
            late_key + jnp.where(inside, early_key, 0.0),
            late_value + jnp.where(inside, early_value, 0.0),
            jnp.minimum(early_depth, late_depth),
        )

    zero_sums = jnp.zeros((upper_count, count_of_rows, feat_width), jnp.float32)
    identity_sums = (zero_sums, zero_sums, jnp.full((1,), float(DEPTH), jnp.float32))
    after_key, after_value, after_depth = entering(
        (send_key, send_value, own_depth.astype(jnp.float32)[None]),
        "node",
        accumulate,
        identity_sums,
    )
    zero_row = jnp.zeros((1, count_of_rows, feat_width), jnp.float32)
    padded_key = jnp.concatenate([after_key, zero_row], axis=0)
    padded_value = jnp.concatenate([after_value, zero_row], axis=0)
    own_mask = own_slot[:, None, None]
    key_grad = jnp.sum(jnp.where(own_mask, key_terms + padded_key, 0.0), axis=0).astype(
        jnp.bfloat16
    )
    value_grad = jnp.sum(jnp.where(own_mask, value_terms + padded_value, 0.0), axis=0).astype(
        jnp.bfloat16
    )
    return (attended, query_grad, key_grad, value_grad)


def solution(mesh):
    return jax.shard_map(
        local,
        mesh=mesh,
        in_specs=(
            P(("leaf", "node"), None),
            P(("leaf", "node"), None),
            P(("leaf", "node"), None),
            P(("leaf", "node"), None),
            P("leaf"),
        ),
        out_specs=(
            P(("leaf", "node"), None),
            P(("leaf", "node"), None),
            P(("leaf", "node"), None),
            P(("leaf", "node"), None),
        ),
        check_vma=False,
    )
```

profile of v0, /device:TPU:1, one launch (start us, length us, event | category | flops | bytes accessed | tf_op | source)
XLA Modules:
  0.0 1772.5 jit_solution(8710700036479952398)
XLA Ops:
  8.7 1.2 dynamic_slice.69
  12.4 221.3 %all-gather.7.cloned.1.call-done = bf16[4096,512]{1,0:T(8,128)(2,1)} async-done(((bf16[128,512]{1,0:T(8,128)(2,1)}), bf16[4096,512]{1,0:T(8,128)(2,1)}) %all-gather.7.cloned.1.call-update) | async-done | bytes 4194320 | tf_op jit(solution)/shard_map/all_gather | solution.py:109
  233.8 2.8 gather_fusion.1
  236.5 235.4 %all-gather.5.cloned.1.call-done = bf16[4096,512]{1,0:T(8,128)(2,1)} async-done(((bf16[128,512]{1,0:T(8,128)(2,1)}), bf16[4096,512]{1,0:T(8,128)(2,1)}) %all-gather.5.cloned.1.call-update) | async-done | bytes 4194320 | tf_op jit(solution)/shard_map/all_gather | solution.py:110
  471.9 2.8 gather_fusion
  480.2 53.8 %while.38 = (s32[]{:T(128)}, bf16[128,4096]{1,0:T(8,128)(2,1)}, bf16[128,4096]{1,0:T(8,128)(2,1)}, f32[512,512]{1,0:T(8,128)}, f32[512,512]{1,0:T(8,128)}, /*ind...) while((s32[]{:T(128)}, bf16[128,4096]{1,0:T(8,128)(2,1)}, ...), condition=%wide.region_4.6_spmd.clone, body=%wide.region_1.0_spmd.clone.sunk | while | flops 811728384 | bytes 21926264 | solution.py:150
  482.7 1.8 fusion.85
  484.7 2.0 fusion.87
  487.8 1.3 fusion.88
  490.3 1.2 fusion.89
  491.5 1.2 fusion.90
  496.2 1.8 fusion.85
  498.1 2.0 fusion.87
  501.3 1.3 fusion.88
  503.8 1.2 fusion.89
  509.6 1.8 fusion.85
  511.6 2.0 fusion.87
  514.7 1.3 fusion.88
  517.2 1.2 fusion.89
  523.0 1.8 fusion.85
  525.0 2.0 fusion.87
  528.1 1.3 fusion.88
  530.6 1.2 fusion.89
  531.9 1.2 fusion.90
  534.1 1.3 slice.18
  535.6 1.4 broadcast_select_fusion.2
  538.2 1.3 dynamic-slice
  540.1 110.2 %all-reduce.2 = f32[32]{0:T(128)S(1)} all-reduce(f32[32]{0:T(128)S(1)} %dynamic-update-slice), channel_id=1, replica_groups=mesh['leaf'=16,'node'=32] {'node'}, use_global_device_ids=true, to_apply=%add.2 | all-reduce | flops 32 | bytes 256
  650.4 461.4 %all-gather.11.cloned.1.call-done = f32[32,3,128,512]{3,2,1,0:T(8,128)} async-done(((f32[1,3,128,512]{3,2,1,0:T(8,128)}), f32[32,3,128,512]{3,2,1,0:T(8,128)}) %all-gather.11.cloned.1.call-update) | async-done | bytes 25165840 | tf_op jit(solution)/shard_map/all_gather | solution.py:12
  1111.7 549.8 %all-gather.9.cloned.1.call-done = f32[32,3,128,512]{3,2,1,0:T(8,128)} async-done(((f32[1,3,128,512]{3,2,1,0:T(8,128)}), f32[32,3,128,512]{3,2,1,0:T(8,128)}) %all-gather.9.cloned.1.call-update) | async-done | bytes 25165840 | tf_op jit(solution)/shard_map/all_gather | solution.py:12
  1661.6 101.9 %while.39 = (s32[]{:T(128)}, f32[3,128,512]{2,1,0:T(8,128)S(1)}, f32[3,128,512]{2,1,0:T(8,128)S(1)}, s32[]{:T(128)}, f32[32,3,128,512]{3,2,1,0:T(8,128)}, /*inde...) while((s32[]{:T(128)}, f32[3,128,512]{2,1,0:T(8,128)S(1)}, ...), condition=%wide.region_6.8_spmd.clone, body=%wide.region_5.7_spmd.clone.sunk | while | flops 1572875 | bytes 4718801 | solution.py:25
  1662.8 2.0 fusion.92
  1665.9 2.0 fusion.92
  1669.1 2.0 fusion.92
  1672.3 2.0 fusion.92
  1675.5 2.0 fusion.92
  1678.7 2.0 fusion.92
  1681.9 2.0 fusion.92
  1685.1 2.0 fusion.92
  1688.2 2.0 fusion.92
  1691.4 2.0 fusion.92
  1694.6 2.0 fusion.92
  1697.8 2.0 fusion.92
  1701.0 2.0 fusion.92
  1704.2 2.0 fusion.92
  1707.4 2.0 fusion.92
  1710.5 2.0 fusion.92
  1713.7 2.0 fusion.92
  1716.9 2.0 fusion.92
  1720.1 2.0 fusion.92
  1723.3 2.0 fusion.92
  1726.5 2.0 fusion.92
  1729.7 2.0 fusion.92
  1732.8 2.0 fusion.92
  1736.0 2.0 fusion.92
  1739.2 2.0 fusion.92
  1742.4 2.0 fusion.92
  1745.6 2.0 fusion.92
  1748.8 2.0 fusion.92
  1752.0 2.0 fusion.92
  1755.1 2.0 fusion.92
  1758.3 2.0 fusion.92
  1761.5 2.0 fusion.92
  1763.5 2.5 select_reduce_fusion
  (155 shorter events, 74.4 us)
Async XLA Ops:
  7.2 226.6 %all-gather.7.cloned.1.call-start = ((), (), s32[]{:S(2)}) async-start(), calls=%async_computation.1 | async-start | bytes 4325376 | tf_op jit(solution)/shard_map/all_gather | solution.py:109
  7.9 464.0 %all-gather.5.cloned.1.call-start = ((), (), s32[]{:S(2)}) async-start(), calls=%async_computation | async-start | bytes 4325376 | tf_op jit(solution)/shard_map/all_gather | solution.py:110
  8.6 1103.1 %all-gather.11.cloned.1.call-start = ((), (), s32[]{:S(2)}) async-start(), calls=%async_computation.3 | async-start | bytes 25952256 | tf_op jit(solution)/shard_map/all_gather | solution.py:12
  482.7 2.0 copy-start
  489.1 2.4 copy-start.1
  496.1 2.0 copy-start
  502.6 2.4 copy-start.1
  509.6 2.0 copy-start
  516.1 2.4 copy-start.1
  523.0 2.0 copy-start
  529.5 2.4 copy-start.1
  534.1 1.5 copy-start.3
  537.0 1124.6 %all-gather.9.cloned.1.call-start = ((), (), s32[]{:S(2)}) async-start(), calls=%async_computation.2 | async-start | bytes 25952256 | tf_op jit(solution)/shard_map/all_gather | solution.py:12
  1661.6 101.9 %copy-start.2 = (f32[512,512]{1,0:T(8,128)S(1)}, f32[512,512]{1,0:T(8,128)}, u32[]{:S(2)}) copy-start(f32[512,512]{1,0:T(8,128)} %get-tuple-element.379) | copy-start | bytes 3145732
Sparse Core Ops, SparseCore 0:
  10.1 223.6 all-gather.6
  235.8 236.0 all-gather.4
  537.1 574.5 all-gather.10
  1113.7 547.8 all-gather.8
where the time goes:
time: 1770 us
  waiting for transfers between devices  1470 us (83%)
  blocking collectives  110 us (6%)
  other arithmetic  89.9 us (5%)
  local copies, waits for them, and re-layouts  51.6 us (3%)
  matrix products  34.7 us (2%)
    all_gather x2, waiting for transfers between devices, entering(): everything = jax.tree.map(lambda part: lax.all_gather(part, axis), array)  1010 us
    all_gather x1, waiting for transfers between devices, local(): lax.all_gather(state_values, 'node', axis=0, tiled=True)  235 us
    all_gather x1, waiting for transfers between devices, local(): lax.all_gather(key_states, 'node', axis=0, tiled=True)  221 us
    unnamed x1, blocking collectives  110 us
    select_n x32, other arithmetic, hop(): return jax.tree.map(lambda a, b: jnp.where(reached, a, b), new, before)  63 us
  transfers between devices with their start and end apart: 4, of which 4 were waited for; matrix products, arithmetic and copies ran while one was open for 0% of the time, Pallas kernels for 0%

commit v1 on v0

v1 whole, which is shorter than its diff:
```python
import jax
import jax.numpy as jnp
from jax import lax
from jax.experimental import pallas as pl
from jax.experimental.pallas import tpu as pltpu
from jax.sharding import PartitionSpec as P

HEAD = 128
TOK = 128
KV_HEADS = 4
GROUP = 8
BLOCKS = 32
ROWS = 4
COLS = 8
UPPER = 3
SLICE = 32
SCALE = HEAD ** -0.5
LOG2E = 1.4426950408889634
NEG = -1e30
F32 = jnp.float32
BF16 = jnp.bfloat16
Z_GROUPS = [[y * COLS + z for z in range(COLS)] for y in range(ROWS)]
Y_GROUPS = [[y * COLS + z for y in range(ROWS)] for z in range(COLS)]


def last_at(depth_ref, start, stop, level, default):
    def step(j, found):
        return jnp.where(depth_ref[j] == level, j, found)

    return lax.fori_loop(start, stop, step, default)


def pick_kernel(depth_ref, node_ref, row_ref, out_ref, sems):
    start = (node_ref[0] // COLS) * COLS
    copies = []
    for level in range(UPPER):
        if level == 0:
            at = 0
        else:
            at = last_at(depth_ref, start, start + COLS, level, start) - start
        copies.append(pltpu.make_async_copy(row_ref.at[at], out_ref.at[level], sems.at[level]))
    for copy in copies:
        copy.start()
    for copy in copies:
        copy.wait()


def pick(depth, node, row):
    return pl.pallas_call(
        pick_kernel,
        out_shape=jax.ShapeDtypeStruct((UPPER,) + row.shape[1:], row.dtype),
        in_specs=[
            pl.BlockSpec(memory_space=pltpu.SMEM),
            pl.BlockSpec(memory_space=pltpu.SMEM),
            pl.BlockSpec(memory_space=pl.ANY),
        ],
        out_specs=pl.BlockSpec(memory_space=pl.ANY),
        scratch_shapes=[pltpu.SemaphoreType.DMA((UPPER,))],
        name="pick",
    )(depth, node, row)


def dot(a, b):
    return jnp.dot(a, b, preferred_element_type=F32)


PAIR = 2


def main_kernel(
    depth_ref, node_ref, q_ref, do_ref, own_ref, row_ref, col_ref,
    att_ref, dq_ref, up_ref, mine_ref,
    kv, sems,
):
    head = pl.program_id(0)
    node = node_ref[0]
    own_depth = depth_ref[node]

    @pl.when(head == 0)
    def _():
        y = node // COLS
        own_copy = pltpu.make_async_copy(own_ref, kv.at[UPPER], sems.at[UPPER])
        own_copy.start()
        for level in range(UPPER):
            if level == 0:
                at = 0
            else:
                at = last_at(depth_ref, 0, node + 1, level, 0)
            at_row = at // COLS

            @pl.when(at_row == y)
            def _():
                pltpu.make_async_copy(row_ref.at[at - at_row * COLS], kv.at[level], sems.at[level]).start()

            @pl.when(at_row != y)
            def _():
                pltpu.make_async_copy(col_ref.at[at_row, level], kv.at[level], sems.at[level]).start()

        for level in range(UPPER):
            pltpu.make_async_copy(row_ref.at[0], kv.at[level], sems.at[level]).wait()
        own_copy.wait()

    kcols = pl.ds(pl.multiple_of(head * HEAD, HEAD), HEAD)
    vcols = pl.ds(pl.multiple_of((KV_HEADS + head) * HEAD, HEAD), HEAD)
    keys = kv[:, :, kcols].reshape((UPPER + 1) * TOK, HEAD)
    values = kv[:, :, vcols].reshape((UPPER + 1) * TOK, HEAD)
    keys_t = keys.T
    values_t = values.T
    width = PAIR * TOK
    u = lax.broadcasted_iota(jnp.int32, (TOK, width), 0)
    t = lax.rem(lax.broadcasted_iota(jnp.int32, (TOK, width), 1), TOK)
    causal = u <= t
    bias = [jnp.where(level < own_depth, 0.0, NEG).astype(F32) for level in range(UPPER)]
    dk = jnp.zeros(((UPPER + 1) * TOK, HEAD), F32)
    dv = jnp.zeros(((UPPER + 1) * TOK, HEAD), F32)
    for pair in range(GROUP // PAIR):
        cols = [pl.ds((pair * PAIR + m) * HEAD, HEAD) for m in range(PAIR)]
        q = jnp.concatenate([q_ref[:, c] for c in cols], axis=0)
        do = jnp.concatenate([do_ref[:, c] for c in cols], axis=0)
        q_t = q.T
        do_t = do.T
        s = dot(keys, q_t)
        parts = [s[level * TOK:(level + 1) * TOK] + bias[level] for level in range(UPPER)]
        parts.append(jnp.where(causal, s[UPPER * TOK:], NEG))
        s = jnp.concatenate(parts, axis=0)
        top = jnp.max(s, axis=0, keepdims=True)
        w = jnp.exp2((s - top) * (SCALE * LOG2E))
        p = w * (1.0 / jnp.sum(w, axis=0, keepdims=True))
        p_low = p.astype(BF16)
        att_t = dot(values_t, p_low).astype(BF16)
        delta = jnp.sum(do_t.astype(F32) * att_t.astype(F32), axis=0, keepdims=True)
        dp = dot(values, do_t)
        ds = (p * (dp - delta)).astype(BF16)
        dq_t = (dot(keys_t, ds) * SCALE).astype(BF16)
        dv = dv + dot(p_low, do)
        dk = dk + dot(ds, q)
        for m in range(PAIR):
            att_ref[:, cols[m]] = att_t[:, m * TOK:(m + 1) * TOK].T
            dq_ref[:, cols[m]] = dq_t[:, m * TOK:(m + 1) * TOK].T
    dk = dk * SCALE
    for which, grad in enumerate((dk, dv)):
        mine_ref[which, 0] = grad[UPPER * TOK:]
        for level in range(UPPER):
            for part in range(TOK // SLICE):
                first = level * TOK + part * SLICE
                up_ref[which, part, pl.ds(level * SLICE, SLICE), :] = grad[first:first + SLICE].astype(BF16)


def attend(depth, node, queries, out_grad, own, row, col):
    wide = pl.BlockSpec((TOK, GROUP * HEAD), lambda h: (0, h))
    parts = TOK // SLICE
    return pl.pallas_call(
        main_kernel,
        grid=(KV_HEADS,),
        out_shape=(
            jax.ShapeDtypeStruct(queries.shape, BF16),
            jax.ShapeDtypeStruct(queries.shape, BF16),
            jax.ShapeDtypeStruct((2, KV_HEADS * parts, UPPER * SLICE, HEAD), BF16),
            jax.ShapeDtypeStruct((2, KV_HEADS, TOK, HEAD), F32),
        ),
        in_specs=[
            pl.BlockSpec(memory_space=pltpu.SMEM),
            pl.BlockSpec(memory_space=pltpu.SMEM),
            wide,
            wide,
            pl.BlockSpec(memory_space=pl.ANY),
            pl.BlockSpec(memory_space=pl.ANY),
            pl.BlockSpec(memory_space=pl.ANY),
        ],
        out_specs=(
            wide,
            wide,
            pl.BlockSpec((2, parts, UPPER * SLICE, HEAD), lambda h: (0, h, 0, 0)),
            pl.BlockSpec((2, 1, TOK, HEAD), lambda h: (0, h, 0, 0)),
        ),
        scratch_shapes=[
            pltpu.VMEM((UPPER + 1, TOK, 2 * KV_HEADS * HEAD), BF16),
            pltpu.SemaphoreType.DMA((UPPER + 1,)),
        ],
        compiler_params=pltpu.CompilerParams(vmem_limit_bytes=32 * 1024 * 1024),
        name="attend",
    )(depth, node, queries, out_grad, own, row, col)


def owner_kernel(depth_ref, in_ref, out_ref, total):
    total[...] = jnp.zeros_like(total)

    def step(i, last):
        last_one, last_two = last
        owners = (0, last_one, last_two)
        for level in range(UPPER):
            piece = in_ref[i, pl.ds(level * SLICE, SLICE), :].astype(F32)
            total[owners[level]] += piece
        depth = depth_ref[i]
        return (jnp.where(depth == 1, i, last_one), jnp.where(depth == 2, i, last_two))

    lax.fori_loop(0, BLOCKS, step, (jnp.int32(0), jnp.int32(0)))
    out_ref[...] = total[...].astype(BF16)


def sum_by_owner(depth, terms):
    return pl.pallas_call(
        owner_kernel,
        out_shape=jax.ShapeDtypeStruct((BLOCKS, SLICE, HEAD), BF16),
        in_specs=[
            pl.BlockSpec(memory_space=pltpu.SMEM),
            pl.BlockSpec(memory_space=pltpu.VMEM),
        ],
        out_specs=pl.BlockSpec(memory_space=pltpu.VMEM),
        scratch_shapes=[pltpu.VMEM((BLOCKS, SLICE, HEAD), F32)],
        compiler_params=pltpu.CompilerParams(vmem_limit_bytes=16 * 1024 * 1024),
        name="sum_by_owner",
    )(depth, terms)


def finish_kernel(below_ref, mine_ref, dk_ref, dv_ref):
    for which, out_ref in enumerate((dk_ref, dv_ref)):
        for head in range(KV_HEADS):
            grad = mine_ref[which, head] + below_ref[which, head].astype(F32)
            out_ref[:, pl.ds(head * HEAD, HEAD)] = grad.astype(BF16)


def finish(below, mine):
    shape = jax.ShapeDtypeStruct((TOK, KV_HEADS * HEAD), BF16)
    return pl.pallas_call(finish_kernel, out_shape=(shape, shape), name="finish")(below, mine)


def local(queries, key_states, state_values, out_grad, block_depth):
    node = lax.axis_index("node").astype(jnp.int32).reshape(1)
    own = jnp.concatenate([key_states, state_values], axis=1)
    row = lax.all_gather(own, "node", axis_index_groups=Z_GROUPS)
    col = lax.all_gather(pick(block_depth, node, row), "node", axis_index_groups=Y_GROUPS)
    attended, query_grad, up, mine = attend(block_depth, node, queries, out_grad, own, row, col)
    up = up.reshape(BLOCKS, UPPER * SLICE, HEAD)
    terms = lax.all_to_all(up, "node", 0, 0)
    sums = sum_by_owner(block_depth, terms)
    below = lax.all_to_all(sums, "node", 0, 0)
    key_grad, value_grad = finish(below.reshape(2, KV_HEADS, TOK, HEAD), mine)
    return attended, query_grad, key_grad, value_grad


def solution(mesh):
    split = P(("leaf", "node"), None)
    return jax.shard_map(
        local,
        mesh=mesh,
        in_specs=(split, split, split, split, P("leaf")),
        out_specs=(split, split, split, split),
        check_vma=False,
    )
```

time: 1770 us -> 262 us (0.15)
  waiting for transfers between devices: 1470 us -> 120 us
  other arithmetic: 89.9 us -> 0 us
  local copies, waits for them, and re-layouts: 51.6 us -> 5.74 us
  Pallas kernels: 0 us -> 45.7 us
  matrix products: 34.7 us -> 0 us
  blocking collectives: 110 us -> 75.8 us
    all_gather x4 -> x2, waiting for transfers between devices: 1470 us -> 120 us  [the longest x1 71.9 us: local(): row = lax.all_gather(own, 'node', axis_index_groups=Z_GROUPS)]
    unnamed x1 -> x0, blocking collectives: 110 us -> none
    all_to_all x0 -> x2, blocking collectives: none -> 75.8 us  [the longest x1 51.6 us: local(): terms = lax.all_to_all(up, 'node', 0, 0)]
    select_n x36 -> x0, other arithmetic: 66.2 us -> none  [the longest x32 63 us: hop(): return jax.tree.map(lambda a, b: jnp.where(reached, a, b), new, before)]
    pallas_call x0 -> x4, Pallas kernels: none -> 45.7 us  [the longest x1 25.9 us: pick(): pl.pallas_call(pick_kernel, out_shape=jax.ShapeDtypeStruct((UPPER,) + row...]
    dynamic_slice x51 -> x0, local copies, waits for them, and re-layouts: 29.8 us -> none  [the longest x32 19 us: hop(): new = combine(before, jax.tree.map(lambda part: part[at], everything))]
    dot_general x20 -> x0, matrix products: 27.6 us -> none  [the longest x4 7.9 us: head_group(): jnp.einsum('jtu,ud->tjd', probs_low, value_cols, preferred_element_type=j...]
    gt x32 -> x0, other arithmetic: 18.7 us -> none  [accumulate(): inside = (late_depth[0] > upper_levels)[:, None, None]]
  transfers between devices with their start and end apart: 4 -> 2, of which waited for: 4 -> 2; matrix products, arithmetic and copies ran while one was open for 0% -> 0% of each run, Pallas kernels for 0% -> 0%
where the time goes in v1:
time: 262 us
  waiting for transfers between devices  120 us (46%)
  blocking collectives  75.8 us (29%)
  Pallas kernels  45.7 us (17%)
  between operations  14.1 us (5%)
  local copies, waits for them, and re-layouts  5.74 us (2%)
    all_gather x1, waiting for transfers between devices, local(): row = lax.all_gather(own, 'node', axis_index_groups=Z_GROUPS)  71.9 us
    all_to_all x1, blocking collectives, local(): terms = lax.all_to_all(up, 'node', 0, 0)  51.6 us
    all_gather x1, waiting for transfers between devices, local(): lax.all_gather(pick(block_depth, node, row), 'node', axis_index_groups=Y_...  48.3 us
    pallas_call x1, Pallas kernels, pick(): pl.pallas_call(pick_kernel, out_shape=jax.ShapeDtypeStruct((UPPER,) + row...  25.9 us
    all_to_all x1, blocking collectives, local(): below = lax.all_to_all(sums, 'node', 0, 0)  24.2 us
    pallas_call x1, Pallas kernels, attend(): pl.pallas_call(main_kernel, grid=(KV_HEADS,), out_shape=(jax.ShapeDtypeSt...  17 us
  transfers between devices with their start and end apart: 2, of which 2 were waited for; matrix products, arithmetic and copies ran while one was open for 0% of the time, Pallas kernels for 0%

profile of v1, /device:TPU:1, one launch (start us, length us, event | category | flops | bytes accessed | tf_op | source)
XLA Modules:
  0.0 261.7 jit_solution(118215321622016823)
XLA Ops:
  7.2 0.0 copy-start.7
  7.2 0.0 copy-start.4
  7.2 0.0 all-gather.5.cloned.1.call-start
  7.2 1.0 constant_dynamic-update-slice_fusion.1
  8.2 0.9 constant_dynamic-update-slice_fusion.own_ref
  9.1 0.0 copy-start.2
  9.2 0.7 copy-done.2
  9.9 0.0 all-gather.5.cloned.1.call-update
  9.9 0.0 copy-start.3
  9.9 0.0 all-gather.7.cloned.1.call-start
  9.9 71.9 %all-gather.5.cloned.1.call-done = bf16[1024,1024]{1,0:T(8,128)(2,1)} async-done(((bf16[128,1024]{1,0:T(8,128)(2,1)}), bf16[1024,1024]{1,0:T(8,128)(2,1)}) %all-gather.5.cloned.1.call-update) | async-done | bytes 2097168 | tf_op jit(solution)/shard_map/all_gather | solution.py:231
  81.8 0.0 copy-start
  81.8 25.9 %pick.1 = bf16[3,128,1024]{2,1,0:T(8,128)(2,1)} custom-call(s32[32]{0:T(128)} %depth_ref.5, s32[1]{0:T(128)} %bitcast.node_ref, bf16[8,128,1024]{2,1,0:T(8,128)(2,1)} %bitcast.5), custom_call_target="tpu_custom_call" | custom-call | tf_op jit(solution)/shard_map/pick/pallas_call | solution.py:49
  107.8 0.0 all-gather.7.cloned.1.call-update
  107.8 48.3 %all-gather.7.cloned.1.call-done = bf16[12,128,1024]{2,1,0:T(8,128)(2,1)} async-done(((bf16[3,128,1024]{2,1,0:T(8,128)(2,1)}), bf16[12,128,1024]{2,1,0:T(8,128)(2,1)}) %all-gather.7.cloned.1.call-update) | async-done | bytes 3145744 | tf_op jit(solution)/shard_map/all_gather | solution.py:232
  156.1 0.0 copy-done.7
  156.1 0.0 copy-done.4
  156.1 0.0 copy-done.3
  156.1 0.0 copy-done
  156.1 0.0 copy-start.1
  156.1 1.9 copy-done.1
  158.0 0.0 copy-start.5
  158.0 1.2 copy-done.5
  159.2 17.0 %attend.1 = (bf16[128,4096]{1,0:T(8,128)(2,1)}, bf16[128,4096]{1,0:T(8,128)(2,1)}, bf16[2,16,96,128]{3,2,1,0:T(8,128)(2,1)S(1)}, f32[2,4,128,128]{3,2,1,0:T(8,128)S(1)}) custom-call(s32[32]{0:T(128)S(1)} %copy-done.7, s32[1]{0:T(128)} %bitcast.node_ref, bf16[128,4096]{1,0:T(8,128)(2,1)S(1)} %copy-done.4, bf16[128,4096]{1,0:T(8,128)(2,1)S(1)} %copy-done.5, ...), custom_call_target="tpu_custom_call" | custom-call | tf_op jit(solution)/shard_map/attend/pallas_call | solution.py:152
  176.1 0.0 copy-start.6
  176.2 51.6 %all_to_all.10.in_ref = bf16[32,96,128]{2,1,0:T(8,128)(2,1)S(1)} all-to-all(bf16[32,96,128]{2,1,0:T(8,128)(2,1)S(1)} %bitcast.8), channel_id=1, replica_groups=mesh['leaf'=16,'node'=32] {'node'}, dimensions={0} | all-to-all | bytes 1572864 | tf_op jit(solution)/shard_map/all_to_all | solution.py:235
  227.7 1.0 sum_by_owner.1
  228.8 24.2 %all_to_all.11 = bf16[32,32,128]{2,1,0:T(8,128)(2,1)} all-to-all(bf16[32,32,128]{2,1,0:T(8,128)(2,1)S(1)} %sum_by_owner.1), channel_id=1, replica_groups=mesh['leaf'=16,'node'=32] {'node'}, dimensions={0} | all-to-all | bytes 524288 | tf_op jit(solution)/shard_map/all_to_all | solution.py:237
  253.0 0.0 copy-done.6
  253.0 1.9 finish.1
Async XLA Ops:
  7.2 148.9 %copy-start.7 = (s32[32]{0:T(128)S(1)}, s32[32]{0:T(128)}, u32[]{:S(2)}) copy-start(s32[32]{0:T(128)} %depth_ref.5) | copy-start | bytes 388
  7.2 148.9 %copy-start.4 = (bf16[128,4096]{1,0:T(8,128)(2,1)S(1)}, bf16[128,4096]{1,0:T(8,128)(2,1)}, u32[]{:S(2)}) copy-start(bf16[128,4096]{1,0:T(8,128)(2,1)} %q_ref.1) | copy-start | bytes 3145732
  7.2 74.7 %all-gather.5.cloned.1.call-start = ((), (), s32[]{:S(2)}) async-start(), calls=%async_computation.2 | async-start | bytes 2359296 | tf_op jit(solution)/shard_map/all_gather | solution.py:231
  9.1 0.7 copy-start.2
  9.9 146.2 %copy-start.3 = (bf16[128,1024]{1,0:T(8,128)(2,1)S(1)}, bf16[128,1024]{1,0:T(8,128)(2,1)}, u32[]{:S(2)}) copy-start(bf16[128,1024]{1,0:T(8,128)(2,1)} %copy-done.2) | copy-start | bytes 786436
  9.9 146.2 %all-gather.7.cloned.1.call-start = ((), (), s32[]{:S(2)}) async-start(), calls=%async_computation.3 | async-start | bytes 3932160 | tf_op jit(solution)/shard_map/all_gather | solution.py:232
  81.8 74.2 %copy-start = (bf16[1024,1024]{1,0:T(8,128)(2,1)S(1)}, bf16[1024,1024]{1,0:T(8,128)(2,1)}, u32[]{:S(2)}) copy-start(bf16[1024,1024]{1,0:T(8,128)(2,1)} %all-gather.5.cloned.1.call-done) | copy-start | bytes 6291460
  156.1 1.9 copy-start.1
  158.0 1.2 copy-start.5
  176.1 76.9 %copy-start.6 = (f32[2,4,128,128]{3,2,1,0:T(8,128)}, f32[2,4,128,128]{3,2,1,0:T(8,128)S(1)}, u32[]{:S(2)}) copy-start(f32[2,4,128,128]{3,2,1,0:T(8,128)S(1)} %get-tuple-element.13.mine_ref) | copy-start | bytes 1572868
Sparse Core Ops, SparseCore 0:
  10.7 71.1 all-gather.4
  107.9 48.0 all-gather.6

commit v2 on v1

v2 whole, which is shorter than its diff:
```python
import jax
import jax.numpy as jnp
from jax import lax
from jax.experimental import pallas as pl
from jax.experimental.pallas import tpu as pltpu
from jax.sharding import PartitionSpec as P

HEAD = 128
TOK = 128
KV_HEADS = 4
GROUP = 8
BLOCKS = 32
ROWS = 4
COLS = 8
QUAD = 4
HALF = ROWS * QUAD
UPPER = 3
SLICE = 2 * KV_HEADS * TOK // HALF
PARTS = TOK // SLICE
ACROSS = 2 * ROWS + 1
SCALE = HEAD ** -0.5
LOG2E = 1.4426950408889634
NEG = -1e30
F32 = jnp.float32
BF16 = jnp.bfloat16
HALVES = [[y * COLS + h * QUAD + q for y in range(ROWS) for q in range(QUAD)] for h in range(COLS // QUAD)]
SWAP = [(node, node ^ QUAD) for node in range(BLOCKS)]
SMEM = pl.BlockSpec(memory_space=pltpu.SMEM)
VMEM = pl.BlockSpec(memory_space=pltpu.VMEM)


def half_of(node):
    return lax.rem(node, COLS) // QUAD


def member_of(node):
    return (node // COLS) * QUAD + lax.rem(node, QUAD)


def across_of(node, level):
    if level == 0:
        return 2 * ROWS
    return (node // COLS) * 2 + level - 1


def last_in_quad(depth_ref, first, level):
    found = first
    for q in range(QUAD):
        found = jnp.where(depth_ref[first + q] == level, first + q, found)
    return found


def cut_kernel(k_ref, v_ref, out_ref):
    for which, ref in enumerate((k_ref, v_ref)):
        for head in range(KV_HEADS):
            for part in range(PARTS):
                out_ref[(which * KV_HEADS + head) * PARTS + part] = ref[
                    pl.ds(part * SLICE, SLICE), pl.ds(head * HEAD, HEAD)
                ]


def cut(keys, values):
    return pl.pallas_call(
        cut_kernel,
        out_shape=jax.ShapeDtypeStruct((HALF, SLICE, HEAD), BF16),
        in_specs=[VMEM, VMEM],
        out_specs=VMEM,
        name="cut",
    )(keys, values)


def summary_kernel(depth_ref, node_ref, held_ref, out_ref):
    half = half_of(node_ref[0])
    for y in range(ROWS):
        first = y * COLS + half * QUAD
        for level in range(1, UPPER):
            at = last_in_quad(depth_ref, first, level)
            out_ref[across_of(first, level)] = held_ref[member_of(at)]
    out_ref[2 * ROWS] = held_ref[0]


def summary(depth, node, held):
    return pl.pallas_call(
        summary_kernel,
        out_shape=jax.ShapeDtypeStruct((ACROSS, SLICE, HEAD), BF16),
        in_specs=[SMEM, SMEM, VMEM],
        out_specs=VMEM,
        name="summary",
    )(depth, node, held)


def path_kernel(depth_ref, node_ref, held_ref, across_ref, out_ref):
    half = half_of(node_ref[0])

    def step(j, last):
        depth = depth_ref[j]
        last = (jnp.where(depth == 1, j, last[0]), jnp.where(depth == 2, j, last[1]))

        @pl.when(half_of(j) == half)
        def _():
            for level in range(UPPER):
                at = jnp.int32(0) if level == 0 else last[level - 1]
                here = half_of(at) == half
                piece = jnp.where(here, held_ref[member_of(at)], across_ref[across_of(at, level)])
                out_ref[member_of(j), pl.ds(level * SLICE, SLICE), :] = piece

        return last

    lax.fori_loop(0, BLOCKS, step, (jnp.int32(0), jnp.int32(0)))


def paths(depth, node, held, across):
    return pl.pallas_call(
        path_kernel,
        out_shape=jax.ShapeDtypeStruct((HALF, UPPER * SLICE, HEAD), BF16),
        in_specs=[SMEM, SMEM, VMEM, VMEM],
        out_specs=VMEM,
        name="paths",
    )(depth, node, held, across)


def dot(a, b):
    return jnp.dot(a, b, preferred_element_type=F32)


PAIR = 2


def main_kernel(
    depth_ref, node_ref, q_ref, do_ref, k_ref, v_ref, ku_ref, vu_ref,
    att_ref, dq_ref, up_ref, mine_ref,
):
    own_depth = depth_ref[node_ref[0]]

    def path_of(upper_ref, own_ref):
        pieces = [
            upper_ref[0, part, pl.ds(level * SLICE, SLICE), :]
            for level in range(UPPER)
            for part in range(PARTS)
        ]
        return jnp.concatenate(pieces + [own_ref[...]], axis=0)

    keys = path_of(ku_ref, k_ref)
    values = path_of(vu_ref, v_ref)
    keys_t = keys.T
    values_t = values.T
    width = PAIR * TOK
    u = lax.broadcasted_iota(jnp.int32, (TOK, width), 0)
    t = lax.rem(lax.broadcasted_iota(jnp.int32, (TOK, width), 1), TOK)
    causal = u <= t
    bias = [jnp.where(level < own_depth, 0.0, NEG).astype(F32) for level in range(UPPER)]
    dk = jnp.zeros(((UPPER + 1) * TOK, HEAD), F32)
    dv = jnp.zeros(((UPPER + 1) * TOK, HEAD), F32)
    for pair in range(GROUP // PAIR):
        cols = [pl.ds((pair * PAIR + m) * HEAD, HEAD) for m in range(PAIR)]
        q = jnp.concatenate([q_ref[:, c] for c in cols], axis=0)
        do = jnp.concatenate([do_ref[:, c] for c in cols], axis=0)
        q_t = q.T
        do_t = do.T
        s = dot(keys, q_t)
        parts = [s[level * TOK:(level + 1) * TOK] + bias[level] for level in range(UPPER)]
        parts.append(jnp.where(causal, s[UPPER * TOK:], NEG))
        s = jnp.concatenate(parts, axis=0)
        top = jnp.max(s, axis=0, keepdims=True)
        w = jnp.exp2((s - top) * (SCALE * LOG2E))
        p = w * (1.0 / jnp.sum(w, axis=0, keepdims=True))
        p_low = p.astype(BF16)
        att_t = dot(values_t, p_low).astype(BF16)
        delta = jnp.sum(do_t.astype(F32) * att_t.astype(F32), axis=0, keepdims=True)
        dp = dot(values, do_t)
        ds = (p * (dp - delta)).astype(BF16)
        dq_t = (dot(keys_t, ds) * SCALE).astype(BF16)
        dv = dv + dot(p_low, do)
        dk = dk + dot(ds, q)
        for m in range(PAIR):
            att_ref[:, cols[m]] = att_t[:, m * TOK:(m + 1) * TOK].T
            dq_ref[:, cols[m]] = dq_t[:, m * TOK:(m + 1) * TOK].T
    dk = dk * SCALE
    for which, grad in enumerate((dk, dv)):
        mine_ref[which, 0] = grad[UPPER * TOK:]
        for level in range(UPPER):
            for part in range(PARTS):
                first = level * TOK + part * SLICE
                up_ref[which, 0, part, pl.ds(level * SLICE, SLICE), :] = grad[first:first + SLICE].astype(BF16)


def attend(depth, node, queries, out_grad, keys, values, upper):
    upper = upper.reshape(2 * KV_HEADS, PARTS, UPPER * SLICE, HEAD)
    wide = pl.BlockSpec((TOK, GROUP * HEAD), lambda h: (0, h))
    narrow = pl.BlockSpec((TOK, HEAD), lambda h: (0, h))
    upper_block = (1, PARTS, UPPER * SLICE, HEAD)
    return pl.pallas_call(
        main_kernel,
        grid=(KV_HEADS,),
        out_shape=(
            jax.ShapeDtypeStruct(queries.shape, BF16),
            jax.ShapeDtypeStruct(queries.shape, BF16),
            jax.ShapeDtypeStruct((2, KV_HEADS, PARTS, UPPER * SLICE, HEAD), BF16),
            jax.ShapeDtypeStruct((2, KV_HEADS, TOK, HEAD), F32),
        ),
        in_specs=[
            SMEM,
            SMEM,
            wide,
            wide,
            narrow,
            narrow,
            pl.BlockSpec(upper_block, lambda h: (h, 0, 0, 0)),
            pl.BlockSpec(upper_block, lambda h: (KV_HEADS + h, 0, 0, 0)),
        ],
        out_specs=(
            wide,
            wide,
            pl.BlockSpec((2,) + upper_block, lambda h: (0, h, 0, 0, 0)),
            pl.BlockSpec((2, 1, TOK, HEAD), lambda h: (0, h, 0, 0)),
        ),
        compiler_params=pltpu.CompilerParams(vmem_limit_bytes=32 * 1024 * 1024),
        name="attend",
    )(depth, node, queries, out_grad, keys, values, upper, upper)


def owner_kernel(depth_ref, node_ref, terms_ref, own_ref, across_ref, across_sum):
    half = half_of(node_ref[0])
    own_ref[...] = jnp.zeros_like(own_ref)
    across_sum[...] = jnp.zeros_like(across_sum)

    def step(j, last):
        @pl.when(half_of(j) == half)
        def _():
            for level in range(UPPER):
                at = jnp.int32(0) if level == 0 else last[level - 1]
                here = half_of(at) == half
                piece = terms_ref[member_of(j), pl.ds(level * SLICE, SLICE), :].astype(F32)
                own_ref[member_of(at)] += jnp.where(here, piece, 0.0)
                across_sum[across_of(at, level)] += jnp.where(here, 0.0, piece)

        depth = depth_ref[j]
        return (jnp.where(depth == 1, j, last[0]), jnp.where(depth == 2, j, last[1]))

    lax.fori_loop(0, BLOCKS, step, (jnp.int32(0), jnp.int32(0)))
    across_ref[...] = across_sum[...].astype(BF16)


def sum_by_owner(depth, node, terms):
    return pl.pallas_call(
        owner_kernel,
        out_shape=(
            jax.ShapeDtypeStruct((HALF, SLICE, HEAD), F32),
            jax.ShapeDtypeStruct((ACROSS, SLICE, HEAD), BF16),
        ),
        in_specs=[SMEM, SMEM, VMEM],
        out_specs=(VMEM, VMEM),
        scratch_shapes=[pltpu.VMEM((ACROSS, SLICE, HEAD), F32)],
        name="sum_by_owner",
    )(depth, node, terms)


def join_kernel(depth_ref, node_ref, own_ref, across_ref, out_ref, total):
    half = half_of(node_ref[0])
    total[...] = own_ref[...]
    for y in range(ROWS):
        first = y * COLS + half * QUAD
        for level in range(1, UPPER):
            at = last_in_quad(depth_ref, first, level)
            total[member_of(at)] += across_ref[across_of(first, level)].astype(F32)
    total[0] += jnp.where(half == 0, across_ref[2 * ROWS].astype(F32), 0.0)
    out_ref[...] = total[...].astype(BF16)


def join(depth, node, own, across):
    return pl.pallas_call(
        join_kernel,
        out_shape=jax.ShapeDtypeStruct((HALF, SLICE, HEAD), BF16),
        in_specs=[SMEM, SMEM, VMEM, VMEM],
        out_specs=VMEM,
        scratch_shapes=[pltpu.VMEM((HALF, SLICE, HEAD), F32)],
        name="join",
    )(depth, node, own, across)


def finish_kernel(below_ref, mine_ref, dk_ref, dv_ref):
    for which, out_ref in enumerate((dk_ref, dv_ref)):
        for head in range(KV_HEADS):
            for part in range(PARTS):
                rows = pl.ds(part * SLICE, SLICE)
                below = below_ref[(which * KV_HEADS + head) * PARTS + part].astype(F32)
                out_ref[rows, pl.ds(head * HEAD, HEAD)] = (mine_ref[which, head, rows, :] + below).astype(BF16)


def finish(below, mine):
    shape = jax.ShapeDtypeStruct((TOK, KV_HEADS * HEAD), BF16)
    return pl.pallas_call(
        finish_kernel,
        out_shape=(shape, shape),
        in_specs=[VMEM, VMEM],
        out_specs=(VMEM, VMEM),
        name="finish",
    )(below, mine)


def exchange(array):
    return lax.all_to_all(array, "node", 0, 0, axis_index_groups=HALVES)


def local(queries, key_states, state_values, out_grad, block_depth):
    node = lax.axis_index("node").astype(jnp.int32).reshape(1)
    held = exchange(cut(key_states, state_values))
    across = lax.ppermute(summary(block_depth, node, held), "node", SWAP)
    upper = exchange(paths(block_depth, node, held, across))
    attended, query_grad, up, mine = attend(
        block_depth, node, queries, out_grad, key_states, state_values, upper
    )
    terms = exchange(up.reshape(HALF, UPPER * SLICE, HEAD))
    own_sum, across_sum = sum_by_owner(block_depth, node, terms)
    across_sum = lax.ppermute(across_sum, "node", SWAP)
    below = exchange(join(block_depth, node, own_sum, across_sum))
    key_grad, value_grad = finish(below, mine)
    return attended, query_grad, key_grad, value_grad


def solution(mesh):
    split = P(("leaf", "node"), None)
    return jax.shard_map(
        local,
        mesh=mesh,
        in_specs=(split, split, split, split, P("leaf")),
        out_specs=(split, split, split, split),
        check_vma=False,
    )
```

time: 262 us -> 162 us (0.62)
  waiting for transfers between devices: 120 us -> 36.1 us
  starting transfers between devices: 0.08 us -> 25.4 us
  Pallas kernels: 45.7 us -> 30.5 us
  between operations: 14.1 us -> 0.68 us
  blocking collectives: 75.8 us -> 64.8 us
    all_gather x2 -> x0, waiting for transfers between devices: 120 us -> none  [the longest x1 71.9 us: local(): row = lax.all_gather(own, 'node', axis_index_groups=Z_GROUPS)]
    ppermute x0 -> x2, waiting for transfers between devices: none -> 26.4 us  [the longest x1 13.5 us: local(): across = lax.ppermute(summary(block_depth, node, held), 'node', SWAP)]
    ppermute x0 -> x2, starting transfers between devices: none -> 16.2 us  [the longest x1 8.82 us: local(): across = lax.ppermute(summary(block_depth, node, held), 'node', SWAP)]
    pallas_call x3 -> x6, Pallas kernels: 28.8 us -> 13.7 us  [the longest x1 3.35 us: sum_by_owner(): pl.pallas_call(owner_kernel, out_shape=(jax.ShapeDtypeStruct((HALF, SLICE...]
    all_to_all x2 -> x3, blocking collectives: 75.8 us -> 64.8 us  [exchange(): return lax.all_to_all(array, 'node', 0, 0, axis_index_groups=HALVES)]
    all_to_all x0 -> x1, waiting for transfers between devices: none -> 9.67 us  [exchange(): return lax.all_to_all(array, 'node', 0, 0, axis_index_groups=HALVES)]
    all_to_all x0 -> x1, starting transfers between devices: none -> 9.19 us  [exchange(): return lax.all_to_all(array, 'node', 0, 0, axis_index_groups=HALVES)]
  transfers between devices with their start and end apart: 2 -> 3, of which waited for: 2 -> 3; matrix products, arithmetic and copies ran while one was open for 0% -> 0% of each run, Pallas kernels for 0% -> 0%
where the time goes in v2:
time: 162 us; the launch traced here: 161 us
  blocking collectives  64.8 us (40%)
  waiting for transfers between devices  36.1 us (22%)
  Pallas kernels  30.5 us (19%)
  starting transfers between devices  25.4 us (16%)
  local copies, waits for them, and re-layouts  3.49 us (2%)
    all_to_all x3, blocking collectives, exchange(): return lax.all_to_all(array, 'node', 0, 0, axis_index_groups=HALVES)  64.8 us
    pallas_call x1, Pallas kernels, attend(): pl.pallas_call(main_kernel, grid=(KV_HEADS,), out_shape=(jax.ShapeDtypeSt...  16.8 us
    ppermute x1, waiting for transfers between devices, local(): across = lax.ppermute(summary(block_depth, node, held), 'node', SWAP)  13.5 us
    ppermute x1, waiting for transfers between devices, local(): across_sum = lax.ppermute(across_sum, 'node', SWAP)  13 us
    all_to_all x1, waiting for transfers between devices, exchange(): return lax.all_to_all(array, 'node', 0, 0, axis_index_groups=HALVES)  9.67 us
    all_to_all x1, starting transfers between devices, exchange(): return lax.all_to_all(array, 'node', 0, 0, axis_index_groups=HALVES)  9.19 us
    ppermute x1, starting transfers between devices, local(): across = lax.ppermute(summary(block_depth, node, held), 'node', SWAP)  8.82 us
    ppermute x1, starting transfers between devices, local(): across_sum = lax.ppermute(across_sum, 'node', SWAP)  7.36 us
  transfers between devices with their start and end apart: 3, of which 3 were waited for; matrix products, arithmetic and copies ran while one was open for 0% of the time, Pallas kernels for 0%

profile of v2, /device:TPU:1, one launch (start us, length us, event | category | flops | bytes accessed | tf_op | source)
XLA Modules:
  0.0 160.9 jit_solution(8042042894447571774)
XLA Ops:
  0.6 1.7 %cut.1 = bf16[16,64,128]{2,1,0:T(8,128)(2,1)} custom-call(bf16[128,512]{1,0:T(8,128)(2,1)} %k_ref.3, bf16[128,512]{1,0:T(8,128)(2,1)} %v_ref.3), custom_call_target="tpu_custom_call" | custom-call | tf_op jit(solution)/shard_map/cut/pallas_call | solution.py:63
  2.3 9.2 %all-to-all-start = ((bf16[16,64,128]{2,1,0:T(8,128)(2,1)}), bf16[16,64,128]{2,1,0:T(8,128)(2,1)S(1)}, u32[]{:S(2)}, u32[]{:S(2)}) async-start(bf16[16,64,128]{2,1,0:T(8,128)(2,1)} %cut.1), calls=%async_computation | async-start | bytes 524288 | tf_op jit(solution)/shard_map/all_to_all | solution.py:302
  11.5 9.7 %all-to-all-done.held_ref = bf16[16,64,128]{2,1,0:T(8,128)(2,1)S(1)} async-done(((bf16[16,64,128]{2,1,0:T(8,128)(2,1)}), bf16[16,64,128]{2,1,0:T(8,128)(2,1)S(1)}, u32[]{:S(2)}, u32[]{:S(2)}) %all-to-all-start) | async-done | bytes 262176 | tf_op jit(solution)/shard_map/all_to_all | solution.py:302
  21.2 0.0 copy-start.6
  21.2 0.7 copy-done.6
  21.9 1.7 %summary.1 = bf16[9,64,128]{2,1,0:T(8,128)(2,1)} custom-call(s32[32]{0:T(128)} %depth_ref.9, s32[1]{0:T(128)} %bitcast.node_ref, bf16[16,64,128]{2,1,0:T(8,128)(2,1)} %copy-done.6), custom_call_target="tpu_custom_call" | custom-call | tf_op jit(solution)/shard_map/summary/pallas_call | solution.py:83
  23.7 8.8 %collective-permute-start = (bf16[9,64,128]{2,1,0:T(8,128)(2,1)}, bf16[9,64,128]{2,1,0:T(8,128)(2,1)S(1)}, u32[]{:S(2)}, u32[]{:S(2)}) collective-permute-start(bf16[9,64,128]{2,1,0:T(8,128)(2,1)} %summary.1), channel_id=1, source_target_pairs={{0,4},{1,5},{2,6},{3,7},{4,0},{5,1},{6,2},{7,3},{8,12},{9,13},{10,... | collective-permute-start | bytes 442376 | tf_op jit(solution)/shard_map/ppermute | solution.py:308
  32.5 13.5 %collective-permute-done.across_ref = bf16[9,64,128]{2,1,0:T(8,128)(2,1)S(1)} collective-permute-done((bf16[9,64,128]{2,1,0:T(8,128)(2,1)}, bf16[9,64,128]{2,1,0:T(8,128)(2,1)S(1)}, u32[]{:S(2)}, u32[]{:S(2)}) %collective-permute-start) | collective-permute-done | bytes 147488 | tf_op jit(solution)/shard_map/ppermute | solution.py:308
  45.9 0.0 copy-start.8
  45.9 0.7 copy-done.8
  46.6 0.0 copy-start.1
  46.6 3.2 %paths.1 = bf16[16,192,128]{2,1,0:T(8,128)(2,1)} custom-call(s32[32]{0:T(128)} %depth_ref.9, s32[1]{0:T(128)} %bitcast.node_ref, bf16[16,64,128]{2,1,0:T(8,128)(2,1)} %copy-done.6, bf16[9,64,128]{2,1,0:T(8,128)(2,1)} %copy-done.8), custom_call_target="tpu_custom_call" | custom-call | tf_op jit(solution)/shard_map/paths/pallas_call | solution.py:113
  49.8 0.0 copy-start
  49.8 0.0 copy-start.3
  49.8 0.0 copy-start.4
  49.8 25.2 %all_to_all.20 = bf16[16,192,128]{2,1,0:T(8,128)(2,1)S(1)} all-to-all(bf16[16,192,128]{2,1,0:T(8,128)(2,1)} %paths.1), channel_id=1, replica_groups={{0,1,2,3,8,9,10,11,16,17,18,19,24,25,26,27},{4,5,6,7,12,13,14,15,20,21,..., dimensions={0} | all-to-all | bytes 1572864 | tf_op jit(solution)/shard_map/all_to_all | solution.py:302
  75.0 0.0 copy-start.5
  75.0 0.0 copy-done.1
  75.0 0.0 copy-done
  75.0 0.0 copy-done.3
  75.0 0.0 copy-done.4
  75.0 0.6 copy-done.5
  75.6 16.8 %attend.1 = (bf16[128,4096]{1,0:T(8,128)(2,1)}, bf16[128,4096]{1,0:T(8,128)(2,1)}, bf16[2,4,2,192,128]{4,3,2,1,0:T(8,128)(2,1)S(1)}, f32[2,4,128,128]{3,2,1,0:T(8,128)S(1)}) custom-call(s32[32]{0:T(128)S(1)} %copy-done.5, s32[1]{0:T(128)} %bitcast.node_ref, bf16[128,4096]{1,0:T(8,128)(2,1)S(1)} %copy-done, bf16[128,4096]{1,0:T(8,128)(2,1)S(1)} %copy-done.1, ...), custom_call_target="tpu_custom_call" | custom-call | tf_op jit(solution)/shard_map/attend/pallas_call | solution.py:192
  92.4 0.0 copy-start.2
  92.4 0.8 copy-done.2
  93.2 25.4 %all_to_all.21.terms_ref = bf16[16,192,128]{2,1,0:T(8,128)(2,1)} all-to-all(bf16[16,192,128]{2,1,0:T(8,128)(2,1)S(1)} %bitcast.5), channel_id=1, replica_groups={{0,1,2,3,8,9,10,11,16,17,18,19,24,25,26,27},{4,5,6,7,12,13,14,15,20,21,..., dimensions={0} | all-to-all | bytes 1572864 | tf_op jit(solution)/shard_map/all_to_all | solution.py:302
  118.6 3.4 %sum_by_owner.1 = (f32[16,64,128]{2,1,0:T(8,128)}, bf16[9,64,128]{2,1,0:T(8,128)(2,1)}) custom-call(s32[32]{0:T(128)} %depth_ref.9, s32[1]{0:T(128)} %bitcast.node_ref, bf16[16,192,128]{2,1,0:T(8,128)(2,1)} %all_to_all.21.terms_ref), custom_call_target="tpu_custom_call" | custom-call | tf_op jit(solution)/shard_map/sum_by_owner/pallas_call | solution.py:245
  122.0 7.4 %collective-permute-start.1 = (bf16[9,64,128]{2,1,0:T(8,128)(2,1)}, bf16[9,64,128]{2,1,0:T(8,128)(2,1)S(1)}, u32[]{:S(2)}, u32[]{:S(2)}) collective-permute-start(bf16[9,64,128]{2,1,0:T(8,128)(2,1)} %get-tuple-element.16), channel_id=1, source_target_pairs={{0,4},{1,5},{2,6},{3,7},{4,0},{5,1},{6,2},{7,3},{8,12},{9,13},{10,... | collective-permute-start | bytes 442376 | tf_op jit(solution)/shard_map/ppermute | solution.py:315
  129.4 13.0 %collective-permute-done.1.across_ref = bf16[9,64,128]{2,1,0:T(8,128)(2,1)S(1)} collective-permute-done((bf16[9,64,128]{2,1,0:T(8,128)(2,1)}, bf16[9,64,128]{2,1,0:T(8,128)(2,1)S(1)}, u32[]{:S(2)}, u32[]{:S(2)}) %collective-permute-start.1) | collective-permute-done | bytes 147488 | tf_op jit(solution)/shard_map/ppermute | solution.py:315
  142.3 0.0 copy-start.7
  142.3 0.7 copy-done.7
  143.0 1.9 %join.1 = bf16[16,64,128]{2,1,0:T(8,128)(2,1)} custom-call(s32[32]{0:T(128)} %depth_ref.9, s32[1]{0:T(128)} %bitcast.node_ref, f32[16,64,128]{2,1,0:T(8,128)} %get-tuple-element.15.own_ref, bf16[9,64,128]{2,1,0:T(8,128)(2,1)} %copy-done.7), custom_call_target="tpu_custom_call" | custom-call | tf_op jit(solution)/shard_map/join/pallas_call | solution.py:271
  144.9 14.1 %all_to_all.22.below_ref = bf16[16,64,128]{2,1,0:T(8,128)(2,1)} all-to-all(bf16[16,64,128]{2,1,0:T(8,128)(2,1)} %join.1), channel_id=1, replica_groups={{0,1,2,3,8,9,10,11,16,17,18,19,24,25,26,27},{4,5,6,7,12,13,14,15,20,21,..., dimensions={0} | all-to-all | bytes 524288 | tf_op jit(solution)/shard_map/all_to_all | solution.py:302
  159.1 1.9 %finish.1 = (bf16[128,512]{1,0:T(8,128)(2,1)}, bf16[128,512]{1,0:T(8,128)(2,1)}) custom-call(bf16[16,64,128]{2,1,0:T(8,128)(2,1)} %all_to_all.22.below_ref, f32[2,4,128,128]{3,2,1,0:T(8,128)} %copy-done.2), custom_call_target="tpu_custom_call" | custom-call | tf_op jit(solution)/shard_map/finish/pallas_call | solution.py:292
Async XLA Ops:
  2.3 18.9 %all-to-all-start = ((bf16[16,64,128]{2,1,0:T(8,128)(2,1)}), bf16[16,64,128]{2,1,0:T(8,128)(2,1)S(1)}, u32[]{:S(2)}, u32[]{:S(2)}) async-start(bf16[16,64,128]{2,1,0:T(8,128)(2,1)} %cut.1), calls=%async_computation | async-start | bytes 524288 | tf_op jit(solution)/shard_map/all_to_all | solution.py:302
  21.2 0.7 copy-start.6
  23.7 22.3 %collective-permute-start = (bf16[9,64,128]{2,1,0:T(8,128)(2,1)}, bf16[9,64,128]{2,1,0:T(8,128)(2,1)S(1)}, u32[]{:S(2)}, u32[]{:S(2)}) collective-permute-start(bf16[9,64,128]{2,1,0:T(8,128)(2,1)} %summary.1), channel_id=1, source_target_pairs={{0,4},{1,5},{2,6},{3,7},{4,0},{5,1},{6,2},{7,3},{8,12},{9,13},{10,... | collective-permute-start | bytes 442376 | tf_op jit(solution)/shard_map/ppermute | solution.py:308
  45.9 0.7 copy-start.8
  46.6 28.4 %copy-start.1 = (bf16[128,4096]{1,0:T(8,128)(2,1)S(1)}, bf16[128,4096]{1,0:T(8,128)(2,1)}, u32[]{:S(2)}) copy-start(bf16[128,4096]{1,0:T(8,128)(2,1)} %do_ref.1) | copy-start | bytes 3145732
  49.8 25.2 %copy-start = (bf16[128,4096]{1,0:T(8,128)(2,1)S(1)}, bf16[128,4096]{1,0:T(8,128)(2,1)}, u32[]{:S(2)}) copy-start(bf16[128,4096]{1,0:T(8,128)(2,1)} %q_ref.1) | copy-start | bytes 3145732
  49.8 25.2 %copy-start.3 = (bf16[128,512]{1,0:T(8,128)(2,1)S(1)}, bf16[128,512]{1,0:T(8,128)(2,1)}, u32[]{:S(2)}) copy-start(bf16[128,512]{1,0:T(8,128)(2,1)} %k_ref.3) | copy-start | bytes 393220
  49.8 25.2 %copy-start.4 = (bf16[128,512]{1,0:T(8,128)(2,1)S(1)}, bf16[128,512]{1,0:T(8,128)(2,1)}, u32[]{:S(2)}) copy-start(bf16[128,512]{1,0:T(8,128)(2,1)} %v_ref.3) | copy-start | bytes 393220
  75.0 0.7 copy-start.5
  92.4 0.8 copy-start.2
  122.0 20.3 %collective-permute-start.1 = (bf16[9,64,128]{2,1,0:T(8,128)(2,1)}, bf16[9,64,128]{2,1,0:T(8,128)(2,1)S(1)}, u32[]{:S(2)}, u32[]{:S(2)}) collective-permute-start(bf16[9,64,128]{2,1,0:T(8,128)(2,1)} %get-tuple-element.16), channel_id=1, source_target_pairs={{0,4},{1,5},{2,6},{3,7},{4,0},{5,1},{6,2},{7,3},{8,12},{9,13},{10,... | collective-permute-start | bytes 442376 | tf_op jit(solution)/shard_map/ppermute | solution.py:315
  142.3 0.7 copy-start.7

commit v3 on v2

--- a/solution.py
+++ b/solution.py
@@ -29,18 +29,40 @@
 VMEM = pl.BlockSpec(memory_space=pltpu.VMEM)
 
 
+def small(vmem_mib=4):
+    return pltpu.CompilerParams(vmem_limit_bytes=vmem_mib * 1024 * 1024)
+
+
 def half_of(node):
-    return lax.rem(node, COLS) // QUAD
+    return (node >> 2) & 1
 
 
 def member_of(node):
-    return (node // COLS) * QUAD + lax.rem(node, QUAD)
+    return ((node >> 3) << 2) | (node & 3)
 
 
 def across_of(node, level):
-    if level == 0:
-        return 2 * ROWS
-    return (node // COLS) * 2 + level - 1
+    return ((node >> 3) << 1) + (level - 1)
+
+
+def slot_of(node, level, half):
+    return jnp.where(half_of(node) == half, member_of(node), HALF + across_of(node, level))
+
+
+def running_last(depth_ref):
+    before, upto = [], []
+    last = (jnp.int32(0), jnp.int32(0))
+    for j in range(BLOCKS):
+        before.append(last)
+        depth = depth_ref[j]
+        last = (jnp.where(depth == 1, j, last[0]), jnp.where(depth == 2, j, last[1]))
+        upto.append(last)
+    return before, upto
+
+
+def of_half(table, member, half):
+    node = (member // QUAD) * COLS + member % QUAD
+    return [jnp.where(half == 0, a, b) for a, b in zip(table[node], table[node + QUAD])]
 
 
 def last_in_quad(depth_ref, first, level):
@@ -65,6 +87,7 @@
         out_shape=jax.ShapeDtypeStruct((HALF, SLICE, HEAD), BF16),
         in_specs=[VMEM, VMEM],
         out_specs=VMEM,
+        compiler_params=small(),
         name="cut",
     )(keys, values)
 
@@ -75,7 +98,7 @@
         first = y * COLS + half * QUAD
         for level in range(1, UPPER):
             at = last_in_quad(depth_ref, first, level)
-            out_ref[across_of(first, level)] = held_ref[member_of(at)]
+            out_ref[2 * y + level - 1] = held_ref[member_of(at)]
     out_ref[2 * ROWS] = held_ref[0]
 
 
@@ -85,28 +108,21 @@
         out_shape=jax.ShapeDtypeStruct((ACROSS, SLICE, HEAD), BF16),
         in_specs=[SMEM, SMEM, VMEM],
         out_specs=VMEM,
+        compiler_params=small(),
         name="summary",
     )(depth, node, held)
 
 
-def path_kernel(depth_ref, node_ref, held_ref, across_ref, out_ref):
+def path_kernel(depth_ref, node_ref, held_ref, across_ref, out_ref, both):
     half = half_of(node_ref[0])
-
-    def step(j, last):
-        depth = depth_ref[j]
-        last = (jnp.where(depth == 1, j, last[0]), jnp.where(depth == 2, j, last[1]))
-
-        @pl.when(half_of(j) == half)
-        def _():
-            for level in range(UPPER):
-                at = jnp.int32(0) if level == 0 else last[level - 1]
-                here = half_of(at) == half
-                piece = jnp.where(here, held_ref[member_of(at)], across_ref[across_of(at, level)])
-                out_ref[member_of(j), pl.ds(level * SLICE, SLICE), :] = piece
-
-        return last
-
-    lax.fori_loop(0, BLOCKS, step, (jnp.int32(0), jnp.int32(0)))
+    both[pl.ds(0, HALF)] = held_ref[...]
+    both[pl.ds(HALF, ACROSS)] = across_ref[...]
+    root = both[jnp.where(half == 0, 0, HALF + 2 * ROWS)]
+    _, upto = running_last(depth_ref)
+    for member in range(HALF):
+        out_ref[member, pl.ds(0, SLICE), :] = root
+        for level, at in enumerate(of_half(upto, member, half), start=1):
+            out_ref[member, pl.ds(level * SLICE, SLICE), :] = both[slot_of(at, level, half)]
 
 
 def paths(depth, node, held, across):
@@ -115,15 +131,14 @@
         out_shape=jax.ShapeDtypeStruct((HALF, UPPER * SLICE, HEAD), BF16),
         in_specs=[SMEM, SMEM, VMEM, VMEM],
         out_specs=VMEM,
+        scratch_shapes=[pltpu.VMEM((HALF + ACROSS, SLICE, HEAD), BF16)],
+        compiler_params=small(),
         name="paths",
     )(depth, node, held, across)
 
 
 def dot(a, b):
     return jnp.dot(a, b, preferred_element_type=F32)
-
-
-PAIR = 2
 
 
 def main_kernel(
@@ -142,40 +157,33 @@
 
     keys = path_of(ku_ref, k_ref)
     values = path_of(vu_ref, v_ref)
-    keys_t = keys.T
-    values_t = values.T
-    width = PAIR * TOK
+    width = GROUP * TOK
     u = lax.broadcasted_iota(jnp.int32, (TOK, width), 0)
-    t = lax.rem(lax.broadcasted_iota(jnp.int32, (TOK, width), 1), TOK)
-    causal = u <= t
-    bias = [jnp.where(level < own_depth, 0.0, NEG).astype(F32) for level in range(UPPER)]
-    dk = jnp.zeros(((UPPER + 1) * TOK, HEAD), F32)
-    dv = jnp.zeros(((UPPER + 1) * TOK, HEAD), F32)
-    for pair in range(GROUP // PAIR):
-        cols = [pl.ds((pair * PAIR + m) * HEAD, HEAD) for m in range(PAIR)]
-        q = jnp.concatenate([q_ref[:, c] for c in cols], axis=0)
-        do = jnp.concatenate([do_ref[:, c] for c in cols], axis=0)
-        q_t = q.T
-        do_t = do.T
-        s = dot(keys, q_t)
-        parts = [s[level * TOK:(level + 1) * TOK] + bias[level] for level in range(UPPER)]
-        parts.append(jnp.where(causal, s[UPPER * TOK:], NEG))
-        s = jnp.concatenate(parts, axis=0)
-        top = jnp.max(s, axis=0, keepdims=True)
-        w = jnp.exp2((s - top) * (SCALE * LOG2E))
-        p = w * (1.0 / jnp.sum(w, axis=0, keepdims=True))
-        p_low = p.astype(BF16)
-        att_t = dot(values_t, p_low).astype(BF16)
-        delta = jnp.sum(do_t.astype(F32) * att_t.astype(F32), axis=0, keepdims=True)
-        dp = dot(values, do_t)
-        ds = (p * (dp - delta)).astype(BF16)
-        dq_t = (dot(keys_t, ds) * SCALE).astype(BF16)
-        dv = dv + dot(p_low, do)
-        dk = dk + dot(ds, q)
-        for m in range(PAIR):
-            att_ref[:, cols[m]] = att_t[:, m * TOK:(m + 1) * TOK].T
-            dq_ref[:, cols[m]] = dq_t[:, m * TOK:(m + 1) * TOK].T
-    dk = dk * SCALE
+    t = lax.broadcasted_iota(jnp.int32, (TOK, width), 1) & (TOK - 1)
+    heads = [pl.ds(m * HEAD, HEAD) for m in range(GROUP)]
+    q = jnp.concatenate([q_ref[:, c] for c in heads], axis=0)
+    do = jnp.concatenate([do_ref[:, c] for c in heads], axis=0)
+    s = dot(keys, q.T)
+    dp = dot(values, do.T)
+    parts = []
+    for level in range(UPPER):
+        bias = jnp.where(level < own_depth, 0.0, NEG).astype(F32)
+        parts.append(s[level * TOK:(level + 1) * TOK] + bias)
+    parts.append(jnp.where(u <= t, s[UPPER * TOK:], NEG))
+    s = jnp.concatenate(parts, axis=0)
+    top = jnp.max(s, axis=0, keepdims=True)
+    w = jnp.exp2((s - top) * (SCALE * LOG2E))
+    p = w * (1.0 / jnp.sum(w, axis=0, keepdims=True))
+    p_low = p.astype(BF16)
+    delta = jnp.sum(p * dp, axis=0, keepdims=True)
+    ds = (p * (dp - delta)).astype(BF16)
+    att_t = dot(values.T, p_low).astype(BF16)
+    dq_t = (dot(keys.T, ds) * SCALE).astype(BF16)
+    dv = dot(p_low, do)
+    dk = dot(ds, q) * SCALE
+    for m, c in enumerate(heads):
+        att_ref[:, c] = att_t[:, m * TOK:(m + 1) * TOK].T
+        dq_ref[:, c] = dq_t[:, m * TOK:(m + 1) * TOK].T
     for which, grad in enumerate((dk, dv)):
         mine_ref[which, 0] = grad[UPPER * TOK:]
         for level in range(UPPER):
@@ -214,31 +222,29 @@
             pl.BlockSpec((2,) + upper_block, lambda h: (0, h, 0, 0, 0)),
             pl.BlockSpec((2, 1, TOK, HEAD), lambda h: (0, h, 0, 0)),
         ),
-        compiler_params=pltpu.CompilerParams(vmem_limit_bytes=32 * 1024 * 1024),
+        compiler_params=small(32),
         name="attend",
     )(depth, node, queries, out_grad, keys, values, upper, upper)
 
 
-def owner_kernel(depth_ref, node_ref, terms_ref, own_ref, across_ref, across_sum):
+def owner_kernel(depth_ref, node_ref, terms_ref, own_ref, across_ref, both):
     half = half_of(node_ref[0])
-    own_ref[...] = jnp.zeros_like(own_ref)
-    across_sum[...] = jnp.zeros_like(across_sum)
-
-    def step(j, last):
-        @pl.when(half_of(j) == half)
-        def _():
-            for level in range(UPPER):
-                at = jnp.int32(0) if level == 0 else last[level - 1]
-                here = half_of(at) == half
-                piece = terms_ref[member_of(j), pl.ds(level * SLICE, SLICE), :].astype(F32)
-                own_ref[member_of(at)] += jnp.where(here, piece, 0.0)
-                across_sum[across_of(at, level)] += jnp.where(here, 0.0, piece)
-
-        depth = depth_ref[j]
-        return (jnp.where(depth == 1, j, last[0]), jnp.where(depth == 2, j, last[1]))
-
-    lax.fori_loop(0, BLOCKS, step, (jnp.int32(0), jnp.int32(0)))
-    across_ref[...] = across_sum[...].astype(BF16)
+    both[...] = jnp.zeros_like(both)
+    before, _ = running_last(depth_ref)
+    root = jnp.zeros((SLICE, HEAD), F32)
+    running = [jnp.zeros((SLICE, HEAD), F32)] * (UPPER - 1)
+    previous = [jnp.int32(0)] * (UPPER - 1)
+    for member in range(HALF):
+        root = root + terms_ref[member, pl.ds(0, SLICE), :].astype(F32)
+        for k, at in enumerate(of_half(before, member, half)):
+            piece = terms_ref[member, pl.ds((k + 1) * SLICE, SLICE), :].astype(F32)
+            running[k] = running[k] * jnp.where(at == previous[k], 1.0, 0.0).astype(F32) + piece
+            previous[k] = at
+            both[slot_of(at, k + 1, half)] = running[k]
+    at_root = jnp.where(half == 0, 0, HALF + 2 * ROWS)
+    both[at_root] = both[at_root] + root
+    own_ref[...] = both[pl.ds(0, HALF)]
+    across_ref[...] = both[pl.ds(HALF, ACROSS)].astype(BF16)
 
 
 def sum_by_owner(depth, node, terms):
@@ -250,21 +256,26 @@
         ),
         in_specs=[SMEM, SMEM, VMEM],
         out_specs=(VMEM, VMEM),
-        scratch_shapes=[pltpu.VMEM((ACROSS, SLICE, HEAD), F32)],
+        scratch_shapes=[pltpu.VMEM((HALF + ACROSS, SLICE, HEAD), F32)],
+        compiler_params=small(),
         name="sum_by_owner",
     )(depth, node, terms)
 
 
-def join_kernel(depth_ref, node_ref, own_ref, across_ref, out_ref, total):
+def join_kernel(depth_ref, node_ref, own_ref, across_ref, out_ref):
     half = half_of(node_ref[0])
-    total[...] = own_ref[...]
     for y in range(ROWS):
         first = y * COLS + half * QUAD
-        for level in range(1, UPPER):
-            at = last_in_quad(depth_ref, first, level)
-            total[member_of(at)] += across_ref[across_of(first, level)].astype(F32)
-    total[0] += jnp.where(half == 0, across_ref[2 * ROWS].astype(F32), 0.0)
-    out_ref[...] = total[...].astype(BF16)
+        lasts = [last_in_quad(depth_ref, first, level) for level in range(1, UPPER)]
+        for q in range(QUAD):
+            total = own_ref[y * QUAD + q]
+            for k, at in enumerate(lasts):
+                chosen = jnp.where(at == first + q, 1.0, 0.0).astype(F32)
+                total = total + across_ref[2 * y + k].astype(F32) * chosen
+            if y == 0 and q == 0:
+                chosen = jnp.where(half == 0, 1.0, 0.0).astype(F32)
+                total = total + across_ref[2 * ROWS].astype(F32) * chosen
+            out_ref[y * QUAD + q] = total.astype(BF16)
 
 
 def join(depth, node, own, across):
@@ -273,7 +284,7 @@
         out_shape=jax.ShapeDtypeStruct((HALF, SLICE, HEAD), BF16),
         in_specs=[SMEM, SMEM, VMEM, VMEM],
         out_specs=VMEM,
-        scratch_shapes=[pltpu.VMEM((HALF, SLICE, HEAD), F32)],
+        compiler_params=small(),
         name="join",
     )(depth, node, own, across)
 
@@ -294,6 +305,7 @@
         out_shape=(shape, shape),
         in_specs=[VMEM, VMEM],
         out_specs=(VMEM, VMEM),
+        compiler_params=small(),
         name="finish",
     )(below, mine)
 

time: 162 us -> 142 us (0.88)
  Pallas kernels: 30.5 us -> 14.6 us
  blocking collectives: 64.8 us -> 62.4 us
  local copies, waits for them, and re-layouts: 3.49 us -> 1.83 us
    pallas_call x1, Pallas kernels: 16.8 us -> 10.4 us  [attend(): pl.pallas_call(main_kernel, grid=(KV_HEADS,), out_shape=(jax.ShapeDtypeSt...]
    pallas_call x1, Pallas kernels: 3.35 us -> 0.82 us  [sum_by_owner(): pl.pallas_call(owner_kernel, out_shape=(jax.ShapeDtypeStruct((HALF, SLICE...]
    pallas_call x1, Pallas kernels: 3.16 us -> 0.74 us  [paths(): pl.pallas_call(path_kernel, out_shape=jax.ShapeDtypeStruct((HALF, UPPER *...]
    all_to_all x3, blocking collectives: 64.8 us -> 62.4 us  [exchange(): return lax.all_to_all(array, 'node', 0, 0, axis_index_groups=HALVES)]
    unnamed x18 -> x14, local copies, waits for them, and re-layouts: 3.49 us -> 1.83 us
where the time goes in v3:
time: 142 us; the launch traced here: 141 us
  blocking collectives  62.4 us (44%)
  waiting for transfers between devices  35.7 us (25%)
  starting transfers between devices  26 us (18%)
  Pallas kernels  14.6 us (10%)
  local copies, waits for them, and re-layouts  1.83 us (1%)
    all_to_all x3, blocking collectives, exchange(): return lax.all_to_all(array, 'node', 0, 0, axis_index_groups=HALVES)  62.4 us
    ppermute x1, waiting for transfers between devices, local(): across = lax.ppermute(summary(block_depth, node, held), 'node', SWAP)  13.3 us
    ppermute x1, waiting for transfers between devices, local(): across_sum = lax.ppermute(across_sum, 'node', SWAP)  12.8 us
    pallas_call x1, Pallas kernels, attend(): pl.pallas_call(main_kernel, grid=(KV_HEADS,), out_shape=(jax.ShapeDtypeSt...  10.4 us
    all_to_all x1, waiting for transfers between devices, exchange(): return lax.all_to_all(array, 'node', 0, 0, axis_index_groups=HALVES)  9.66 us
    all_to_all x1, starting transfers between devices, exchange(): return lax.all_to_all(array, 'node', 0, 0, axis_index_groups=HALVES)  9.19 us
    ppermute x1, starting transfers between devices, local(): across = lax.ppermute(summary(block_depth, node, held), 'node', SWAP)  8.83 us
    ppermute x1, starting transfers between devices, local(): across_sum = lax.ppermute(across_sum, 'node', SWAP)  8.02 us
  transfers between devices with their start and end apart: 3, of which 3 were waited for; matrix products, arithmetic and copies ran while one was open for 0% of the time, Pallas kernels for 0%

profile of v3, /device:TPU:1, one launch (start us, length us, event | category | flops | bytes accessed | tf_op | source)
XLA Modules:
  0.0 141.4 jit_solution(14702980624039487526)
XLA Ops:
  0.6 0.0 copy-start.2
  0.6 0.9 copy-done.2
  1.5 0.0 copy-start.4
  1.5 0.9 copy-done.4
  2.4 0.7 cut.1
  3.2 9.2 %all-to-all-start = ((bf16[16,64,128]{2,1,0:T(8,128)(2,1)}), bf16[16,64,128]{2,1,0:T(8,128)(2,1)S(1)}, u32[]{:S(2)}, u32[]{:S(2)}) async-start(bf16[16,64,128]{2,1,0:T(8,128)(2,1)} %cut.1), calls=%async_computation | async-start | bytes 524288 | tf_op jit(solution)/shard_map/all_to_all | solution.py:314
  12.4 0.0 copy-start.6
  12.4 9.7 %all-to-all-done.held_ref = bf16[16,64,128]{2,1,0:T(8,128)(2,1)S(1)} async-done(((bf16[16,64,128]{2,1,0:T(8,128)(2,1)}), bf16[16,64,128]{2,1,0:T(8,128)(2,1)S(1)}, u32[]{:S(2)}, u32[]{:S(2)}) %all-to-all-start) | async-done | bytes 262176 | tf_op jit(solution)/shard_map/all_to_all | solution.py:314
  22.1 0.0 copy-done.6
  22.1 0.6 summary.1
  22.7 8.8 %collective-permute-start = (bf16[9,64,128]{2,1,0:T(8,128)(2,1)S(1)}, bf16[9,64,128]{2,1,0:T(8,128)(2,1)S(1)}, u32[]{:S(2)}, u32[]{:S(2)}) collective-permute-start(bf16[9,64,128]{2,1,0:T(8,128)(2,1)S(1)} %summary.1), channel_id=1, source_target_pairs={{0,4},{1,5},{2,6},{3,7},{4,0},{5,1},{6,2},{7,3},{8,12},{9,13},{10,... | collective-permute-start | bytes 442376 | tf_op jit(solution)/shard_map/ppermute | solution.py:320
  31.5 13.3 %collective-permute-done.across_ref = bf16[9,64,128]{2,1,0:T(8,128)(2,1)S(1)} collective-permute-done((bf16[9,64,128]{2,1,0:T(8,128)(2,1)S(1)}, bf16[9,64,128]{2,1,0:T(8,128)(2,1)S(1)}, u32[]{:S(2)}, u32[]{:S(2)}) %collective-permute-start) | collective-permute-done | bytes 147488 | tf_op jit(solution)/shard_map/ppermute | solution.py:320
  44.8 0.0 copy-start.1
  44.8 0.7 paths.1
  45.5 0.0 copy-start
  45.5 0.0 copy-start.3
  45.5 0.0 copy-start.5
  45.5 24.8 %all_to_all.20 = bf16[16,192,128]{2,1,0:T(8,128)(2,1)S(1)} all-to-all(bf16[16,192,128]{2,1,0:T(8,128)(2,1)S(1)} %paths.1), channel_id=1, replica_groups={{0,1,2,3,8,9,10,11,16,17,18,19,24,25,26,27},{4,5,6,7,12,13,14,15,20,21,..., dimensions={0} | all-to-all | bytes 1572864 | tf_op jit(solution)/shard_map/all_to_all | solution.py:314
  70.3 0.0 copy-done.1
  70.3 0.0 copy-done
  70.3 0.0 copy-done.3
  70.3 0.0 copy-done.5
  70.3 10.4 %attend.1 = (bf16[128,4096]{1,0:T(8,128)(2,1)}, bf16[128,4096]{1,0:T(8,128)(2,1)}, bf16[2,4,2,192,128]{4,3,2,1,0:T(8,128)(2,1)S(1)}, f32[2,4,128,128]{3,2,1,0:T(8,128)S(1)}) custom-call(s32[32]{0:T(128)S(1)} %copy-done.6, s32[1]{0:T(128)} %bitcast.node_ref, bf16[128,4096]{1,0:T(8,128)(2,1)S(1)} %copy-done, bf16[128,4096]{1,0:T(8,128)(2,1)S(1)} %copy-done.1, ...), custom_call_target="tpu_custom_call" | custom-call | tf_op jit(solution)/shard_map/attend/pallas_call | solution.py:200
  80.7 24.9 %all_to_all.21.terms_ref = bf16[16,192,128]{2,1,0:T(8,128)(2,1)S(1)} all-to-all(bf16[16,192,128]{2,1,0:T(8,128)(2,1)S(1)} %bitcast.5), channel_id=1, replica_groups={{0,1,2,3,8,9,10,11,16,17,18,19,24,25,26,27},{4,5,6,7,12,13,14,15,20,21,..., dimensions={0} | all-to-all | bytes 1572864 | tf_op jit(solution)/shard_map/all_to_all | solution.py:314
  105.6 0.8 sum_by_owner.1
  106.4 8.0 %collective-permute-start.1 = (bf16[9,64,128]{2,1,0:T(8,128)(2,1)S(1)}, bf16[9,64,128]{2,1,0:T(8,128)(2,1)S(1)}, u32[]{:S(2)}, u32[]{:S(2)}) collective-permute-start(bf16[9,64,128]{2,1,0:T(8,128)(2,1)S(1)} %get-tuple-element.16), channel_id=1, source_target_pairs={{0,4},{1,5},{2,6},{3,7},{4,0},{5,1},{6,2},{7,3},{8,12},{9,13},{10,... | collective-permute-start | bytes 442376 | tf_op jit(solution)/shard_map/ppermute | solution.py:327
  114.4 12.8 %collective-permute-done.1.across_ref = bf16[9,64,128]{2,1,0:T(8,128)(2,1)S(1)} collective-permute-done((bf16[9,64,128]{2,1,0:T(8,128)(2,1)S(1)}, bf16[9,64,128]{2,1,0:T(8,128)(2,1)S(1)}, u32[]{:S(2)}, u32[]{:S(2)}) %collective-permute-start.1) | collective-permute-done | bytes 147488 | tf_op jit(solution)/shard_map/ppermute | solution.py:327
  127.2 0.6 join.1
  127.8 12.8 %all_to_all.22.below_ref = bf16[16,64,128]{2,1,0:T(8,128)(2,1)S(1)} all-to-all(bf16[16,64,128]{2,1,0:T(8,128)(2,1)S(1)} %join.1), channel_id=1, replica_groups={{0,1,2,3,8,9,10,11,16,17,18,19,24,25,26,27},{4,5,6,7,12,13,14,15,20,21,..., dimensions={0} | all-to-all | bytes 524288 | tf_op jit(solution)/shard_map/all_to_all | solution.py:314
  140.6 0.7 finish.1
Async XLA Ops:
  0.6 0.9 copy-start.2
  1.5 0.9 copy-start.4
  3.2 18.9 %all-to-all-start = ((bf16[16,64,128]{2,1,0:T(8,128)(2,1)}), bf16[16,64,128]{2,1,0:T(8,128)(2,1)S(1)}, u32[]{:S(2)}, u32[]{:S(2)}) async-start(bf16[16,64,128]{2,1,0:T(8,128)(2,1)} %cut.1), calls=%async_computation | async-start | bytes 524288 | tf_op jit(solution)/shard_map/all_to_all | solution.py:314
  12.4 9.7 %copy-start.6 = (s32[32]{0:T(128)S(1)}, s32[32]{0:T(128)}, u32[]{:S(2)}) copy-start(s32[32]{0:T(128)} %depth_ref.9) | copy-start | bytes 388
  22.7 22.1 %collective-permute-start = (bf16[9,64,128]{2,1,0:T(8,128)(2,1)S(1)}, bf16[9,64,128]{2,1,0:T(8,128)(2,1)S(1)}, u32[]{:S(2)}, u32[]{:S(2)}) collective-permute-start(bf16[9,64,128]{2,1,0:T(8,128)(2,1)S(1)} %summary.1), channel_id=1, source_target_pairs={{0,4},{1,5},{2,6},{3,7},{4,0},{5,1},{6,2},{7,3},{8,12},{9,13},{10,... | collective-permute-start | bytes 442376 | tf_op jit(solution)/shard_map/ppermute | solution.py:320
  44.8 25.6 %copy-start.1 = (bf16[128,4096]{1,0:T(8,128)(2,1)S(1)}, bf16[128,4096]{1,0:T(8,128)(2,1)}, u32[]{:S(2)}) copy-start(bf16[128,4096]{1,0:T(8,128)(2,1)} %do_ref.1) | copy-start | bytes 3145732
  45.5 24.8 %copy-start = (bf16[128,4096]{1,0:T(8,128)(2,1)S(1)}, bf16[128,4096]{1,0:T(8,128)(2,1)}, u32[]{:S(2)}) copy-start(bf16[128,4096]{1,0:T(8,128)(2,1)} %q_ref.1) | copy-start | bytes 3145732
  45.5 24.8 %copy-start.3 = (bf16[128,512]{1,0:T(8,128)(2,1)S(1)}, bf16[128,512]{1,0:T(8,128)(2,1)}, u32[]{:S(2)}) copy-start(bf16[128,512]{1,0:T(8,128)(2,1)} %k_ref.3) | copy-start | bytes 393220
  45.5 24.8 %copy-start.5 = (bf16[128,512]{1,0:T(8,128)(2,1)S(1)}, bf16[128,512]{1,0:T(8,128)(2,1)}, u32[]{:S(2)}) copy-start(bf16[128,512]{1,0:T(8,128)(2,1)} %v_ref.3) | copy-start | bytes 393220
  106.4 20.8 %collective-permute-start.1 = (bf16[9,64,128]{2,1,0:T(8,128)(2,1)S(1)}, bf16[9,64,128]{2,1,0:T(8,128)(2,1)S(1)}, u32[]{:S(2)}, u32[]{:S(2)}) collective-permute-start(bf16[9,64,128]{2,1,0:T(8,128)(2,1)S(1)} %get-tuple-element.16), channel_id=1, source_target_pairs={{0,4},{1,5},{2,6},{3,7},{4,0},{5,1},{6,2},{7,3},{8,12},{9,13},{10,... | collective-permute-start | bytes 442376 | tf_op jit(solution)/shard_map/ppermute | solution.py:327

commit v4 on v3

--- a/solution.py
+++ b/solution.py
@@ -23,8 +23,16 @@
 NEG = -1e30
 F32 = jnp.float32
 BF16 = jnp.bfloat16
-HALVES = [[y * COLS + h * QUAD + q for y in range(ROWS) for q in range(QUAD)] for h in range(COLS // QUAD)]
-SWAP = [(node, node ^ QUAD) for node in range(BLOCKS)]
+ORDER = (
+    (2, 2), (1, 1), (0, 0), (0, 1), (2, 1), (1, 0), (1, 2), (0, 2),
+    (0, 3), (3, 3), (2, 3), (1, 3), (3, 0), (2, 0), (3, 1), (3, 2),
+)
+HALVES = [
+    [y * COLS + q for y, q in ORDER],
+    [y * COLS + COLS - 1 - q for y, q in ORDER],
+]
+MEMBER = {node: member for half in HALVES for member, node in enumerate(half)}
+SWAP = [(node, node - node % COLS + COLS - 1 - node % COLS) for node in range(BLOCKS)]
 SMEM = pl.BlockSpec(memory_space=pltpu.SMEM)
 VMEM = pl.BlockSpec(memory_space=pltpu.VMEM)
 
@@ -37,57 +45,62 @@
     return (node >> 2) & 1
 
 
-def member_of(node):
-    return ((node >> 3) << 2) | (node & 3)
-
-
-def across_of(node, level):
-    return ((node >> 3) << 1) + (level - 1)
-
-
-def slot_of(node, level, half):
-    return jnp.where(half_of(node) == half, member_of(node), HALF + across_of(node, level))
-
-
-def running_last(depth_ref):
+def slot(node, level, half):
+    if node % COLS // QUAD == half:
+        return MEMBER[node]
+    return HALF + 2 * (node // COLS) + level - 1
+
+
+def last_slots(depth_ref, half):
+    last = [jnp.where(half == 0, slot(0, level, 0), slot(0, level, 1)) for level in range(1, UPPER)]
     before, upto = [], []
-    last = (jnp.int32(0), jnp.int32(0))
-    for j in range(BLOCKS):
-        before.append(last)
-        depth = depth_ref[j]
-        last = (jnp.where(depth == 1, j, last[0]), jnp.where(depth == 2, j, last[1]))
-        upto.append(last)
+    for node in range(BLOCKS):
+        before.append(list(last))
+        for level in range(1, UPPER):
+            here = jnp.where(half == 0, slot(node, level, 0), slot(node, level, 1))
+            last[level - 1] = jnp.where(depth_ref[node] == level, here, last[level - 1])
+        upto.append(list(last))
     return before, upto
 
 
-def of_half(table, member, half):
-    node = (member // QUAD) * COLS + member % QUAD
+def of_half(table, node, half):
     return [jnp.where(half == 0, a, b) for a, b in zip(table[node], table[node + QUAD])]
 
 
-def last_in_quad(depth_ref, first, level):
-    found = first
+def member_at(y, q, half):
+    return jnp.where(half == 0, MEMBER[y * COLS + q], MEMBER[y * COLS + QUAD + q])
+
+
+def last_in_quad(depth_ref, y, level, half):
+    found = member_at(y, 0, half)
     for q in range(QUAD):
-        found = jnp.where(depth_ref[first + q] == level, first + q, found)
+        depth = jnp.where(half == 0, depth_ref[y * COLS + q], depth_ref[y * COLS + QUAD + q])
+        found = jnp.where(depth == level, member_at(y, q, half), found)
     return found
 
 
-def cut_kernel(k_ref, v_ref, out_ref):
+def cut_kernel(k_ref, v_ref, out_ref, sems):
+    copies = []
     for which, ref in enumerate((k_ref, v_ref)):
         for head in range(KV_HEADS):
             for part in range(PARTS):
-                out_ref[(which * KV_HEADS + head) * PARTS + part] = ref[
-                    pl.ds(part * SLICE, SLICE), pl.ds(head * HEAD, HEAD)
-                ]
+                at = (which * KV_HEADS + head) * PARTS + part
+                source = ref.at[pl.ds(part * SLICE, SLICE), pl.ds(head * HEAD, HEAD)]
+                copies.append(pltpu.make_async_copy(source, out_ref.at[at], sems.at[at]))
+    for copy in copies:
+        copy.start()
+    for copy in copies:
+        copy.wait()
 
 
 def cut(keys, values):
     return pl.pallas_call(
         cut_kernel,
         out_shape=jax.ShapeDtypeStruct((HALF, SLICE, HEAD), BF16),
-        in_specs=[VMEM, VMEM],
+        in_specs=[pl.BlockSpec(memory_space=pltpu.HBM)] * 2,
         out_specs=VMEM,
-        compiler_params=small(),
+        scratch_shapes=[pltpu.SemaphoreType.DMA((HALF,))],
+        compiler_params=small(60),
         name="cut",
     )(keys, values)
 
@@ -95,11 +108,9 @@
 def summary_kernel(depth_ref, node_ref, held_ref, out_ref):
     half = half_of(node_ref[0])
     for y in range(ROWS):
-        first = y * COLS + half * QUAD
         for level in range(1, UPPER):
-            at = last_in_quad(depth_ref, first, level)
-            out_ref[2 * y + level - 1] = held_ref[member_of(at)]
-    out_ref[2 * ROWS] = held_ref[0]
+            out_ref[2 * y + level - 1] = held_ref[last_in_quad(depth_ref, y, level, half)]
+    out_ref[2 * ROWS] = held_ref[MEMBER[0]]
 
 
 def summary(depth, node, held):
@@ -117,12 +128,14 @@
     half = half_of(node_ref[0])
     both[pl.ds(0, HALF)] = held_ref[...]
     both[pl.ds(HALF, ACROSS)] = across_ref[...]
-    root = both[jnp.where(half == 0, 0, HALF + 2 * ROWS)]
-    _, upto = running_last(depth_ref)
-    for member in range(HALF):
-        out_ref[member, pl.ds(0, SLICE), :] = root
-        for level, at in enumerate(of_half(upto, member, half), start=1):
-            out_ref[member, pl.ds(level * SLICE, SLICE), :] = both[slot_of(at, level, half)]
+    root = both[jnp.where(half == 0, MEMBER[0], HALF + 2 * ROWS)]
+    _, upto = last_slots(depth_ref, half)
+    for y in range(ROWS):
+        for q in range(QUAD):
+            member = member_at(y, q, half)
+            out_ref[member, pl.ds(0, SLICE), :] = root
+            for level, at in enumerate(of_half(upto, y * COLS + q, half), start=1):
+                out_ref[member, pl.ds(level * SLICE, SLICE), :] = both[at]
 
 
 def paths(depth, node, held, across):
@@ -230,18 +243,21 @@
 def owner_kernel(depth_ref, node_ref, terms_ref, own_ref, across_ref, both):
     half = half_of(node_ref[0])
     both[...] = jnp.zeros_like(both)
-    before, _ = running_last(depth_ref)
+    before, _ = last_slots(depth_ref, half)
     root = jnp.zeros((SLICE, HEAD), F32)
     running = [jnp.zeros((SLICE, HEAD), F32)] * (UPPER - 1)
-    previous = [jnp.int32(0)] * (UPPER - 1)
-    for member in range(HALF):
-        root = root + terms_ref[member, pl.ds(0, SLICE), :].astype(F32)
-        for k, at in enumerate(of_half(before, member, half)):
-            piece = terms_ref[member, pl.ds((k + 1) * SLICE, SLICE), :].astype(F32)
-            running[k] = running[k] * jnp.where(at == previous[k], 1.0, 0.0).astype(F32) + piece
-            previous[k] = at
-            both[slot_of(at, k + 1, half)] = running[k]
-    at_root = jnp.where(half == 0, 0, HALF + 2 * ROWS)
+    previous = before[0]
+    for y in range(ROWS):
+        for q in range(QUAD):
+            member = member_at(y, q, half)
+            root = root + terms_ref[member, pl.ds(0, SLICE), :].astype(F32)
+            owners = of_half(before, y * COLS + q, half)
+            for k, at in enumerate(owners):
+                piece = terms_ref[member, pl.ds((k + 1) * SLICE, SLICE), :].astype(F32)
+                running[k] = running[k] * jnp.where(at == previous[k], 1.0, 0.0).astype(F32) + piece
+                both[at] = running[k]
+            previous = owners
+    at_root = jnp.where(half == 0, MEMBER[0], HALF + 2 * ROWS)
     both[at_root] = both[at_root] + root
     own_ref[...] = both[pl.ds(0, HALF)]
     across_ref[...] = both[pl.ds(HALF, ACROSS)].astype(BF16)
@@ -265,17 +281,17 @@
 def join_kernel(depth_ref, node_ref, own_ref, across_ref, out_ref):
     half = half_of(node_ref[0])
     for y in range(ROWS):
-        first = y * COLS + half * QUAD
-        lasts = [last_in_quad(depth_ref, first, level) for level in range(1, UPPER)]
+        lasts = [last_in_quad(depth_ref, y, level, half) for level in range(1, UPPER)]
         for q in range(QUAD):
-            total = own_ref[y * QUAD + q]
+            member = member_at(y, q, half)
+            total = own_ref[member]
             for k, at in enumerate(lasts):
-                chosen = jnp.where(at == first + q, 1.0, 0.0).astype(F32)
+                chosen = jnp.where(at == member, 1.0, 0.0).astype(F32)
                 total = total + across_ref[2 * y + k].astype(F32) * chosen
             if y == 0 and q == 0:
                 chosen = jnp.where(half == 0, 1.0, 0.0).astype(F32)
                 total = total + across_ref[2 * ROWS].astype(F32) * chosen
-            out_ref[y * QUAD + q] = total.astype(BF16)
+            out_ref[member] = total.astype(BF16)
 
 
 def join(depth, node, own, across):

time: 142 us -> 129 us (0.908); the launches traced: 141 us -> 127 us
  waiting for transfers between devices: 35.7 us -> 13.7 us
  blocking collectives: 62.4 us -> 69.6 us
  local copies, waits for them, and re-layouts: 1.83 us -> 0.03 us
    ppermute x1, waiting for transfers between devices: 13.3 us -> 2.82 us  [local(): across = lax.ppermute(summary(block_depth, node, held), 'node', SWAP)]
    all_to_all x3, blocking collectives: 62.4 us -> 69.6 us  [exchange(): return lax.all_to_all(array, 'node', 0, 0, axis_index_groups=HALVES)]
    ppermute x1, waiting for transfers between devices: 12.8 us -> 6.81 us  [local(): across_sum = lax.ppermute(across_sum, 'node', SWAP)]
    all_to_all x1, waiting for transfers between devices: 9.66 us -> 4.08 us  [exchange(): return lax.all_to_all(array, 'node', 0, 0, axis_index_groups=HALVES)]
    ppermute x1, starting transfers between devices: 8.02 us -> 5.94 us  [local(): across_sum = lax.ppermute(across_sum, 'node', SWAP)]
    ppermute x1, starting transfers between devices: 8.83 us -> 10.9 us  [local(): across = lax.ppermute(summary(block_depth, node, held), 'node', SWAP)]
    unnamed x14 -> x10, local copies, waits for them, and re-layouts: 1.83 us -> 0.03 us
where the time goes in v4:
time: 129 us; the launch traced here: 127 us
  blocking collectives  69.6 us (54%)
  starting transfers between devices  27 us (21%)
  Pallas kernels  15.6 us (12%)
  waiting for transfers between devices  13.7 us (11%)
    all_to_all x3, blocking collectives, exchange(): return lax.all_to_all(array, 'node', 0, 0, axis_index_groups=HALVES)  69.6 us
    ppermute x1, starting transfers between devices, local(): across = lax.ppermute(summary(block_depth, node, held), 'node', SWAP)  10.9 us
    pallas_call x1, Pallas kernels, attend(): pl.pallas_call(main_kernel, grid=(KV_HEADS,), out_shape=(jax.ShapeDtypeSt...  10.4 us
    all_to_all x1, starting transfers between devices, exchange(): return lax.all_to_all(array, 'node', 0, 0, axis_index_groups=HALVES)  10.1 us
    ppermute x1, waiting for transfers between devices, local(): across_sum = lax.ppermute(across_sum, 'node', SWAP)  6.81 us
    ppermute x1, starting transfers between devices, local(): across_sum = lax.ppermute(across_sum, 'node', SWAP)  5.94 us
    all_to_all x1, waiting for transfers between devices, exchange(): return lax.all_to_all(array, 'node', 0, 0, axis_index_groups=HALVES)  4.08 us
    ppermute x1, waiting for transfers between devices, local(): across = lax.ppermute(summary(block_depth, node, held), 'node', SWAP)  2.82 us
  transfers between devices with their start and end apart: 3, of which 3 were waited for; matrix products, arithmetic and copies ran while one was open for 0% of the time, Pallas kernels for 0%

profile of v4, /device:TPU:1, one launch (start us, length us, event | category | flops | bytes accessed | tf_op | source)
XLA Modules:
  0.0 126.5 jit_solution(3901953664493310528)
XLA Ops:
  0.6 1.7 %cut.1 = bf16[16,64,128]{2,1,0:T(8,128)(2,1)} custom-call(bf16[128,512]{1,0:T(8,128)(2,1)} %k_ref.3, bf16[128,512]{1,0:T(8,128)(2,1)} %v_ref.3), custom_call_target="tpu_custom_call" | custom-call | tf_op jit(solution)/shard_map/cut/pallas_call | solution.py:97
  2.4 10.1 %all-to-all-start = ((bf16[16,64,128]{2,1,0:T(8,128)(2,1)}), bf16[16,64,128]{2,1,0:T(8,128)(2,1)S(1)}, u32[]{:S(2)}, u32[]{:S(2)}) async-start(bf16[16,64,128]{2,1,0:T(8,128)(2,1)} %cut.1), calls=%async_computation | async-start | bytes 524288 | tf_op jit(solution)/shard_map/all_to_all | solution.py:330
  12.5 0.0 copy-start.4
  12.5 4.1 %all-to-all-done.held_ref = bf16[16,64,128]{2,1,0:T(8,128)(2,1)S(1)} async-done(((bf16[16,64,128]{2,1,0:T(8,128)(2,1)}), bf16[16,64,128]{2,1,0:T(8,128)(2,1)S(1)}, u32[]{:S(2)}, u32[]{:S(2)}) %all-to-all-start) | async-done | bytes 262176 | tf_op jit(solution)/shard_map/all_to_all | solution.py:330
  16.6 0.0 copy-done.4
  16.6 0.6 summary.1
  17.2 10.9 %collective-permute-start = (bf16[9,64,128]{2,1,0:T(8,128)(2,1)S(1)}, bf16[9,64,128]{2,1,0:T(8,128)(2,1)S(1)}, u32[]{:S(2)}, u32[]{:S(2)}) collective-permute-start(bf16[9,64,128]{2,1,0:T(8,128)(2,1)S(1)} %summary.1), channel_id=1, source_target_pairs={{0,7},{1,6},{2,5},{3,4},{4,3},{5,2},{6,1},{7,0},{8,15},{9,14},{10,... | collective-permute-start | bytes 442376 | tf_op jit(solution)/shard_map/ppermute | solution.py:336
  28.1 2.8 %collective-permute-done.across_ref = bf16[9,64,128]{2,1,0:T(8,128)(2,1)S(1)} collective-permute-done((bf16[9,64,128]{2,1,0:T(8,128)(2,1)S(1)}, bf16[9,64,128]{2,1,0:T(8,128)(2,1)S(1)}, u32[]{:S(2)}, u32[]{:S(2)}) %collective-permute-start) | collective-permute-done | bytes 147488 | tf_op jit(solution)/shard_map/ppermute | solution.py:336
  30.9 0.0 copy-start.1
  30.9 0.7 paths.1
  31.6 0.0 copy-start
  31.6 0.0 copy-start.2
  31.6 0.0 copy-start.3
  31.7 31.8 %all_to_all.20 = bf16[16,192,128]{2,1,0:T(8,128)(2,1)S(1)} all-to-all(bf16[16,192,128]{2,1,0:T(8,128)(2,1)S(1)} %paths.1), channel_id=1, replica_groups={{18,9,0,1,17,8,10,2,3,27,19,11,24,16,25,26},{21,14,7,6,22,15,13,5,4,28,..., dimensions={0} | all-to-all | bytes 1572864 | tf_op jit(solution)/shard_map/all_to_all | solution.py:330
  63.5 0.0 copy-done.1
  63.5 0.0 copy-done
  63.5 0.0 copy-done.2
  63.5 0.0 copy-done.3
  63.5 10.4 %attend.1 = (bf16[128,4096]{1,0:T(8,128)(2,1)}, bf16[128,4096]{1,0:T(8,128)(2,1)}, bf16[2,4,2,192,128]{4,3,2,1,0:T(8,128)(2,1)S(1)}, f32[2,4,128,128]{3,2,1,0:T(8,128)S(1)}) custom-call(s32[32]{0:T(128)S(1)} %copy-done.4, s32[1]{0:T(128)} %bitcast.node_ref, bf16[128,4096]{1,0:T(8,128)(2,1)S(1)} %copy-done, bf16[128,4096]{1,0:T(8,128)(2,1)S(1)} %copy-done.1, ...), custom_call_target="tpu_custom_call" | custom-call | tf_op jit(solution)/shard_map/attend/pallas_call | solution.py:213
  73.9 23.0 %all_to_all.21.terms_ref = bf16[16,192,128]{2,1,0:T(8,128)(2,1)S(1)} all-to-all(bf16[16,192,128]{2,1,0:T(8,128)(2,1)S(1)} %bitcast.5), channel_id=1, replica_groups={{18,9,0,1,17,8,10,2,3,27,19,11,24,16,25,26},{21,14,7,6,22,15,13,5,4,28,..., dimensions={0} | all-to-all | bytes 1572864 | tf_op jit(solution)/shard_map/all_to_all | solution.py:330
  96.9 0.8 sum_by_owner.1
  97.6 5.9 %collective-permute-start.1 = (bf16[9,64,128]{2,1,0:T(8,128)(2,1)S(1)}, bf16[9,64,128]{2,1,0:T(8,128)(2,1)S(1)}, u32[]{:S(2)}, u32[]{:S(2)}) collective-permute-start(bf16[9,64,128]{2,1,0:T(8,128)(2,1)S(1)} %get-tuple-element.16), channel_id=1, source_target_pairs={{0,7},{1,6},{2,5},{3,4},{4,3},{5,2},{6,1},{7,0},{8,15},{9,14},{10,... | collective-permute-start | bytes 442376 | tf_op jit(solution)/shard_map/ppermute | solution.py:343
  103.6 6.8 %collective-permute-done.1.across_ref = bf16[9,64,128]{2,1,0:T(8,128)(2,1)S(1)} collective-permute-done((bf16[9,64,128]{2,1,0:T(8,128)(2,1)S(1)}, bf16[9,64,128]{2,1,0:T(8,128)(2,1)S(1)}, u32[]{:S(2)}, u32[]{:S(2)}) %collective-permute-start.1) | collective-permute-done | bytes 147488 | tf_op jit(solution)/shard_map/ppermute | solution.py:343
  110.4 0.7 join.1
  111.1 14.7 %all_to_all.22.below_ref = bf16[16,64,128]{2,1,0:T(8,128)(2,1)S(1)} all-to-all(bf16[16,64,128]{2,1,0:T(8,128)(2,1)S(1)} %join.1), channel_id=1, replica_groups={{18,9,0,1,17,8,10,2,3,27,19,11,24,16,25,26},{21,14,7,6,22,15,13,5,4,28,..., dimensions={0} | all-to-all | bytes 524288 | tf_op jit(solution)/shard_map/all_to_all | solution.py:330
  125.8 0.7 finish.1
Async XLA Ops:
  2.4 14.2 %all-to-all-start = ((bf16[16,64,128]{2,1,0:T(8,128)(2,1)}), bf16[16,64,128]{2,1,0:T(8,128)(2,1)S(1)}, u32[]{:S(2)}, u32[]{:S(2)}) async-start(bf16[16,64,128]{2,1,0:T(8,128)(2,1)} %cut.1), calls=%async_computation | async-start | bytes 524288 | tf_op jit(solution)/shard_map/all_to_all | solution.py:330
  12.5 4.1 %copy-start.4 = (s32[32]{0:T(128)S(1)}, s32[32]{0:T(128)}, u32[]{:S(2)}) copy-start(s32[32]{0:T(128)} %depth_ref.9) | copy-start | bytes 388
  17.2 13.7 %collective-permute-start = (bf16[9,64,128]{2,1,0:T(8,128)(2,1)S(1)}, bf16[9,64,128]{2,1,0:T(8,128)(2,1)S(1)}, u32[]{:S(2)}, u32[]{:S(2)}) collective-permute-start(bf16[9,64,128]{2,1,0:T(8,128)(2,1)S(1)} %summary.1), channel_id=1, source_target_pairs={{0,7},{1,6},{2,5},{3,4},{4,3},{5,2},{6,1},{7,0},{8,15},{9,14},{10,... | collective-permute-start | bytes 442376 | tf_op jit(solution)/shard_map/ppermute | solution.py:336
  30.9 32.6 %copy-start.1 = (bf16[128,4096]{1,0:T(8,128)(2,1)S(1)}, bf16[128,4096]{1,0:T(8,128)(2,1)}, u32[]{:S(2)}) copy-start(bf16[128,4096]{1,0:T(8,128)(2,1)} %do_ref.1) | copy-start | bytes 3145732
  31.6 31.9 %copy-start = (bf16[128,4096]{1,0:T(8,128)(2,1)S(1)}, bf16[128,4096]{1,0:T(8,128)(2,1)}, u32[]{:S(2)}) copy-start(bf16[128,4096]{1,0:T(8,128)(2,1)} %q_ref.1) | copy-start | bytes 3145732
  31.6 31.9 %copy-start.2 = (bf16[128,512]{1,0:T(8,128)(2,1)S(1)}, bf16[128,512]{1,0:T(8,128)(2,1)}, u32[]{:S(2)}) copy-start(bf16[128,512]{1,0:T(8,128)(2,1)} %k_ref.3) | copy-start | bytes 393220
  31.6 31.9 %copy-start.3 = (bf16[128,512]{1,0:T(8,128)(2,1)S(1)}, bf16[128,512]{1,0:T(8,128)(2,1)}, u32[]{:S(2)}) copy-start(bf16[128,512]{1,0:T(8,128)(2,1)} %v_ref.3) | copy-start | bytes 393220
  97.6 12.8 %collective-permute-start.1 = (bf16[9,64,128]{2,1,0:T(8,128)(2,1)S(1)}, bf16[9,64,128]{2,1,0:T(8,128)(2,1)S(1)}, u32[]{:S(2)}, u32[]{:S(2)}) collective-permute-start(bf16[9,64,128]{2,1,0:T(8,128)(2,1)S(1)} %get-tuple-element.16), channel_id=1, source_target_pairs={{0,7},{1,6},{2,5},{3,4},{4,3},{5,2},{6,1},{7,0},{8,15},{9,14},{10,... | collective-permute-start | bytes 442376 | tf_op jit(solution)/shard_map/ppermute | solution.py:343

commit v5 on v4

v5 whole, which is shorter than its diff:
```python
import jax
import jax.numpy as jnp
from jax import lax
from jax.experimental import pallas as pl
from jax.experimental.pallas import tpu as pltpu
from jax.sharding import PartitionSpec as P

HEAD = 128
TOK = 128
KV_HEADS = 4
GROUP = 8
BLOCKS = 32
ROWS = 4
COLS = 8
QUAD = 4
HALF = ROWS * QUAD
UPPER = 3
SLICE = 2 * KV_HEADS * TOK // HALF
PARTS = TOK // SLICE
ACROSS = 2 * ROWS + 1
ACROSS_BACK = 2 * (ROWS - 1)
SCALE = HEAD ** -0.5
LOG2E = 1.4426950408889634
NEG = -1e30
F32 = jnp.float32
BF16 = jnp.bfloat16
ORDER = (
    (2, 2), (1, 1), (0, 0), (0, 1), (2, 1), (1, 0), (1, 2), (0, 2),
    (0, 3), (3, 3), (2, 3), (1, 3), (3, 0), (2, 0), (3, 1), (3, 2),
)
HALVES = [
    [y * COLS + q for y, q in ORDER],
    [y * COLS + COLS - 1 - q for y, q in ORDER],
]
MEMBER = {node: member for half in HALVES for member, node in enumerate(half)}
TO_SECOND = list(zip(HALVES[0], HALVES[1]))
TO_FIRST = list(zip(HALVES[1], HALVES[0]))
SMEM = pl.BlockSpec(memory_space=pltpu.SMEM)
VMEM = pl.BlockSpec(memory_space=pltpu.VMEM)


def small(vmem_mib=4):
    return pltpu.CompilerParams(vmem_limit_bytes=vmem_mib * 1024 * 1024)


def half_of(node):
    return (node >> 2) & 1


def slot(node, level, half):
    if node % COLS // QUAD == half:
        return MEMBER[node]
    return HALF + 2 * (node // COLS) + level - 1


def last_slots(depth_ref, half):
    last = [jnp.where(half == 0, slot(0, level, 0), slot(0, level, 1)) for level in range(1, UPPER)]
    before, upto = [], []
    for node in range(BLOCKS):
        before.append(list(last))
        for level in range(1, UPPER):
            here = jnp.where(half == 0, slot(node, level, 0), slot(node, level, 1))
            last[level - 1] = jnp.where(depth_ref[node] == level, here, last[level - 1])
        upto.append(list(last))
    return before, upto


def of_half(table, node, half):
    return [jnp.where(half == 0, a, b) for a, b in zip(table[node], table[node + QUAD])]


def member_at(y, q, half):
    return jnp.where(half == 0, MEMBER[y * COLS + q], MEMBER[y * COLS + QUAD + q])


def last_in_quad(depth_ref, y, level, half):
    found = member_at(y, 0, half)
    for q in range(QUAD):
        depth = jnp.where(half == 0, depth_ref[y * COLS + q], depth_ref[y * COLS + QUAD + q])
        found = jnp.where(depth == level, member_at(y, q, half), found)
    return found


def cut_kernel(k_ref, v_ref, out_ref, sems):
    copies = []
    for which, ref in enumerate((k_ref, v_ref)):
        for head in range(KV_HEADS):
            for part in range(PARTS):
                at = (which * KV_HEADS + head) * PARTS + part
                source = ref.at[pl.ds(part * SLICE, SLICE), pl.ds(head * HEAD, HEAD)]
                copies.append(pltpu.make_async_copy(source, out_ref.at[at], sems.at[at]))
    for copy in copies:
        copy.start()
    for copy in copies:
        copy.wait()


def cut(keys, values):
    return pl.pallas_call(
        cut_kernel,
        out_shape=jax.ShapeDtypeStruct((HALF, SLICE, HEAD), BF16),
        in_specs=[pl.BlockSpec(memory_space=pltpu.HBM)] * 2,
        out_specs=VMEM,
        scratch_shapes=[pltpu.SemaphoreType.DMA((HALF,))],
        compiler_params=small(60),
        name="cut",
    )(keys, values)


def summary_kernel(depth_ref, node_ref, held_ref, second_ref, first_ref):
    half = half_of(node_ref[0])
    for y in range(ROWS):
        for level in range(1, UPPER):
            piece = held_ref[last_in_quad(depth_ref, y, level, half)]
            second_ref[2 * y + level - 1] = piece
            if y < ROWS - 1:
                first_ref[2 * y + level - 1] = piece
    second_ref[2 * ROWS] = held_ref[MEMBER[0]]


def summary(depth, node, held):
    return pl.pallas_call(
        summary_kernel,
        out_shape=(
            jax.ShapeDtypeStruct((ACROSS, SLICE, HEAD), BF16),
            jax.ShapeDtypeStruct((ACROSS_BACK, SLICE, HEAD), BF16),
        ),
        in_specs=[SMEM, SMEM, VMEM],
        out_specs=(VMEM, VMEM),
        compiler_params=small(),
        name="summary",
    )(depth, node, held)


def path_kernel(depth_ref, node_ref, held_ref, in_second_ref, in_first_ref, out_ref, both):
    half = half_of(node_ref[0])
    both[pl.ds(0, HALF)] = held_ref[...]

    @pl.when(half == 0)
    def _():
        both[pl.ds(HALF, ACROSS_BACK)] = in_first_ref[...]

    @pl.when(half != 0)
    def _():
        both[pl.ds(HALF, ACROSS)] = in_second_ref[...]

    root = both[jnp.where(half == 0, MEMBER[0], HALF + 2 * ROWS)]
    _, upto = last_slots(depth_ref, half)
    for y in range(ROWS):
        for q in range(QUAD):
            member = member_at(y, q, half)
            out_ref[member, pl.ds(0, SLICE), :] = root
            for level, at in enumerate(of_half(upto, y * COLS + q, half), start=1):
                out_ref[member, pl.ds(level * SLICE, SLICE), :] = both[at]


def paths(depth, node, held, in_second, in_first):
    return pl.pallas_call(
        path_kernel,
        out_shape=jax.ShapeDtypeStruct((HALF, UPPER * SLICE, HEAD), BF16),
        in_specs=[SMEM, SMEM, VMEM, VMEM, VMEM],
        out_specs=VMEM,
        scratch_shapes=[pltpu.VMEM((HALF + ACROSS, SLICE, HEAD), BF16)],
        compiler_params=small(),
        name="paths",
    )(depth, node, held, in_second, in_first)


def dot(a, b):
    return jnp.dot(a, b, preferred_element_type=F32)


def path_of(upper_ref, own_ref, which, head):
    pieces = [
        upper_ref[which * KV_HEADS + head, part, pl.ds(level * SLICE, SLICE), :]
        for level in range(UPPER)
        for part in range(PARTS)
    ]
    return jnp.concatenate(pieces + [own_ref[:, pl.ds(head * HEAD, HEAD)]], axis=0)


def main_kernel(
    depth_ref, node_ref, q_ref, do_ref, k_ref, v_ref, upper_ref,
    att_ref, dq_ref, up_ref, mine_ref,
):
    own_depth = depth_ref[node_ref[0]]
    u = lax.broadcasted_iota(jnp.int32, (TOK, TOK), 0)
    t = lax.broadcasted_iota(jnp.int32, (TOK, TOK), 1)
    biases = [jnp.where(level < own_depth, 0.0, NEG).astype(F32) for level in range(UPPER)]

    def columns(head):
        return [pl.ds((head * GROUP + m) * HEAD, HEAD) for m in range(GROUP)]

    def scores_of(head):
        keys, values = path_of(upper_ref, k_ref, 0, head), path_of(upper_ref, v_ref, 1, head)
        q = jnp.concatenate([q_ref[:, c] for c in columns(head)], axis=0)
        do = jnp.concatenate([do_ref[:, c] for c in columns(head)], axis=0)
        return keys, values, q, do, dot(keys, q.T), dot(values, do.T)

    def probs_of(scores, dprobs):
        p_low, ds = [], []
        for m in range(GROUP):
            s, dp = scores[:, m * TOK:(m + 1) * TOK], dprobs[:, m * TOK:(m + 1) * TOK]
            parts = [s[level * TOK:(level + 1) * TOK] + bias for level, bias in enumerate(biases)]
            parts.append(jnp.where(u <= t, s[UPPER * TOK:], NEG))
            s = jnp.concatenate(parts, axis=0)
            top = jnp.max(s, axis=0, keepdims=True)
            w = jnp.exp2((s - top) * (SCALE * LOG2E))
            p = w * (1.0 / jnp.sum(w, axis=0, keepdims=True))
            delta = jnp.sum(p * dp, axis=0, keepdims=True)
            p_low.append(p.astype(BF16))
            ds.append((p * (dp - delta)).astype(BF16))
        return jnp.concatenate(p_low, axis=1), jnp.concatenate(ds, axis=1)

    later = scores_of(0)
    for head in range(KV_HEADS):
        keys, values, q, do, scores, dprobs = later
        if head + 1 < KV_HEADS:
            later = scores_of(head + 1)
        p_low, ds = probs_of(scores, dprobs)
        att_t = dot(values.T, p_low).astype(BF16)
        dq_t = (dot(keys.T, ds) * SCALE).astype(BF16)
        dv = dot(p_low, do)
        dk = dot(ds, q) * SCALE
        for m, c in enumerate(columns(head)):
            att_ref[:, c] = att_t[:, m * TOK:(m + 1) * TOK].T
            dq_ref[:, c] = dq_t[:, m * TOK:(m + 1) * TOK].T
        for which, grad in enumerate((dk, dv)):
            mine_ref[which, head] = grad[UPPER * TOK:]
            for level in range(UPPER):
                for part in range(PARTS):
                    first = level * TOK + part * SLICE
                    piece = grad[first:first + SLICE].astype(BF16)
                    up_ref[which * KV_HEADS + head, part, pl.ds(level * SLICE, SLICE), :] = piece


def attend(depth, node, queries, out_grad, keys, values, upper):
    upper = upper.reshape(2 * KV_HEADS, PARTS, UPPER * SLICE, HEAD)
    return pl.pallas_call(
        main_kernel,
        out_shape=(
            jax.ShapeDtypeStruct(queries.shape, BF16),
            jax.ShapeDtypeStruct(queries.shape, BF16),
            jax.ShapeDtypeStruct(upper.shape, BF16),
            jax.ShapeDtypeStruct((2, KV_HEADS, TOK, HEAD), F32),
        ),
        in_specs=[SMEM, SMEM] + [VMEM] * 5,
        out_specs=(VMEM,) * 4,
        compiler_params=small(40),
        name="attend",
    )(depth, node, queries, out_grad, keys, values, upper)


def owner_kernel(depth_ref, node_ref, terms_ref, own_ref, first_ref, second_ref, both):
    half = half_of(node_ref[0])
    both[...] = jnp.zeros_like(both)
    before, _ = last_slots(depth_ref, half)
    root = jnp.zeros((SLICE, HEAD), F32)
    running = [jnp.zeros((SLICE, HEAD), F32)] * (UPPER - 1)
    previous = before[0]
    for y in range(ROWS):
        for q in range(QUAD):
            member = member_at(y, q, half)
            root = root + terms_ref[member, pl.ds(0, SLICE), :].astype(F32)
            owners = of_half(before, y * COLS + q, half)
            for k, at in enumerate(owners):
                piece = terms_ref[member, pl.ds((k + 1) * SLICE, SLICE), :].astype(F32)
                running[k] = running[k] * jnp.where(at == previous[k], 1.0, 0.0).astype(F32) + piece
                both[at] = running[k]
            previous = owners
    at_root = jnp.where(half == 0, MEMBER[0], HALF + 2 * ROWS)
    both[at_root] = both[at_root] + root
    own_ref[...] = both[pl.ds(0, HALF)]
    first_ref[...] = both[pl.ds(HALF, ACROSS)].astype(BF16)
    second_ref[...] = both[pl.ds(HALF, ACROSS_BACK)].astype(BF16)


def sum_by_owner(depth, node, terms):
    return pl.pallas_call(
        owner_kernel,
        out_shape=(
            jax.ShapeDtypeStruct((HALF, SLICE, HEAD), F32),
            jax.ShapeDtypeStruct((ACROSS, SLICE, HEAD), BF16),
            jax.ShapeDtypeStruct((ACROSS_BACK, SLICE, HEAD), BF16),
        ),
        in_specs=[SMEM, SMEM, VMEM],
        out_specs=(VMEM, VMEM, VMEM),
        scratch_shapes=[pltpu.VMEM((HALF + ACROSS, SLICE, HEAD), F32)],
        compiler_params=small(),
        name="sum_by_owner",
    )(depth, node, terms)


def join_kernel(depth_ref, node_ref, own_ref, in_first_ref, in_second_ref, out_ref):
    half = half_of(node_ref[0])
    for y in range(ROWS):
        lasts = [last_in_quad(depth_ref, y, level, half) for level in range(1, UPPER)]
        for q in range(QUAD):
            member = member_at(y, q, half)
            total = own_ref[member]
            for k, at in enumerate(lasts):
                chosen = jnp.where(at == member, 1.0, 0.0).astype(F32)
                piece = in_first_ref[2 * y + k].astype(F32)
                if y < ROWS - 1:
                    piece = piece + in_second_ref[2 * y + k].astype(F32)
                total = total + piece * chosen
            if y == 0 and q == 0:
                total = total + in_first_ref[2 * ROWS].astype(F32)
            out_ref[member] = total.astype(BF16)


def join(depth, node, own, in_first, in_second):
    return pl.pallas_call(
        join_kernel,
        out_shape=jax.ShapeDtypeStruct((HALF, SLICE, HEAD), BF16),
        in_specs=[SMEM, SMEM, VMEM, VMEM, VMEM],
        out_specs=VMEM,
        compiler_params=small(),
        name="join",
    )(depth, node, own, in_first, in_second)


def finish_kernel(below_ref, mine_ref, dk_ref, dv_ref):
    for which, out_ref in enumerate((dk_ref, dv_ref)):
        for head in range(KV_HEADS):
            for part in range(PARTS):
                rows = pl.ds(part * SLICE, SLICE)
                below = below_ref[(which * KV_HEADS + head) * PARTS + part].astype(F32)
                out_ref[rows, pl.ds(head * HEAD, HEAD)] = (mine_ref[which, head, rows, :] + below).astype(BF16)


def finish(below, mine):
    shape = jax.ShapeDtypeStruct((TOK, KV_HEADS * HEAD), BF16)
    return pl.pallas_call(
        finish_kernel,
        out_shape=(shape, shape),
        in_specs=[VMEM, VMEM],
        out_specs=(VMEM, VMEM),
        compiler_params=small(),
        name="finish",
    )(below, mine)


def exchange(array):
    return lax.all_to_all(array, "node", 0, 0, axis_index_groups=HALVES)


def local(queries, key_states, state_values, out_grad, block_depth):
    node = lax.axis_index("node").astype(jnp.int32).reshape(1)
    held = exchange(cut(key_states, state_values))
    for_second, for_first = summary(block_depth, node, held)
    in_second = lax.ppermute(for_second, "node", TO_SECOND)
    in_first = lax.ppermute(for_first, "node", TO_FIRST)
    upper = exchange(paths(block_depth, node, held, in_second, in_first))
    attended, query_grad, up, mine = attend(
        block_depth, node, queries, out_grad, key_states, state_values, upper
    )
    terms = exchange(up.reshape(HALF, UPPER * SLICE, HEAD))
    own_sum, for_first, for_second = sum_by_owner(block_depth, node, terms)
    in_first = lax.ppermute(for_first, "node", TO_FIRST)
    in_second = lax.ppermute(for_second, "node", TO_SECOND)
    below = exchange(join(block_depth, node, own_sum, in_first, in_second))
    key_grad, value_grad = finish(below, mine)
    return attended, query_grad, key_grad, value_grad


def solution(mesh):
    split = P(("leaf", "node"), None)
    return jax.shard_map(
        local,
        mesh=mesh,
        in_specs=(split, split, split, split, P("leaf")),
        out_specs=(split, split, split, split),
        check_vma=False,
    )
```

time: 129 us -> 128 us (level)
  blocking collectives: 69.6 us -> 59.4 us
  starting transfers between devices: 27 us -> 34.2 us
  waiting for transfers between devices: 13.7 us -> 16.6 us
    all_to_all x3, blocking collectives: 69.6 us -> 59.4 us  [exchange(): return lax.all_to_all(array, 'node', 0, 0, axis_index_groups=HALVES)]
    ppermute x2 -> x4, starting transfers between devices: 16.8 us -> 24.1 us  [the longest x2 21.5 us: local(): in_second = lax.ppermute(for_second, 'node', TO_SECOND)]
    ppermute x2 -> x4, waiting for transfers between devices: 9.62 us -> 12.5 us  [the longest x2 10.9 us: local(): in_first = lax.ppermute(for_first, 'node', TO_FIRST)]
  transfers between devices with their start and end apart: 3 -> 5, of which waited for: 3 -> 3; matrix products, arithmetic and copies ran while one was open for 0% -> 0% of each run, Pallas kernels for 0% -> 0%
where the time goes in v5:
time: 128 us; the launch traced here: 126 us
  blocking collectives  59.4 us (46%)
  starting transfers between devices  34.2 us (27%)
  waiting for transfers between devices  16.6 us (13%)
  Pallas kernels  14.9 us (12%)
    all_to_all x3, blocking collectives, exchange(): return lax.all_to_all(array, 'node', 0, 0, axis_index_groups=HALVES)  59.4 us
    ppermute x2, starting transfers between devices, local(): in_second = lax.ppermute(for_second, 'node', TO_SECOND)  21.5 us
    ppermute x2, waiting for transfers between devices, local(): in_first = lax.ppermute(for_first, 'node', TO_FIRST)  10.9 us
    all_to_all x1, starting transfers between devices, exchange(): return lax.all_to_all(array, 'node', 0, 0, axis_index_groups=HALVES)  10.1 us
    pallas_call x1, Pallas kernels, attend(): pl.pallas_call(main_kernel, out_shape=(jax.ShapeDtypeStruct(queries.shape...  9.66 us
    all_to_all x1, waiting for transfers between devices, exchange(): return lax.all_to_all(array, 'node', 0, 0, axis_index_groups=HALVES)  4.08 us
    ppermute x2, starting transfers between devices, local(): in_first = lax.ppermute(for_first, 'node', TO_FIRST)  2.58 us
  transfers between devices with their start and end apart: 5, of which 3 were waited for; matrix products, arithmetic and copies ran while one was open for 0% of the time, Pallas kernels for 0%

profile of v5, /device:TPU:1, one launch (start us, length us, event | category | flops | bytes accessed | tf_op | source)
XLA Modules:
  0.0 125.8 jit_solution(6892674116441496518)
XLA Ops:
  0.6 1.7 %cut.1 = bf16[16,64,128]{2,1,0:T(8,128)(2,1)} custom-call(bf16[128,512]{1,0:T(8,128)(2,1)} %k_ref.3, bf16[128,512]{1,0:T(8,128)(2,1)} %v_ref.3), custom_call_target="tpu_custom_call" | custom-call | tf_op jit(solution)/shard_map/cut/pallas_call | solution.py:99
  2.4 10.1 %all-to-all-start = ((bf16[16,64,128]{2,1,0:T(8,128)(2,1)}), bf16[16,64,128]{2,1,0:T(8,128)(2,1)S(1)}, u32[]{:S(2)}, u32[]{:S(2)}) async-start(bf16[16,64,128]{2,1,0:T(8,128)(2,1)} %cut.1), calls=%async_computation | async-start | bytes 524288 | tf_op jit(solution)/shard_map/all_to_all | solution.py:345
  12.5 0.0 copy-start.4
  12.5 4.1 %all-to-all-done.held_ref = bf16[16,64,128]{2,1,0:T(8,128)(2,1)S(1)} async-done(((bf16[16,64,128]{2,1,0:T(8,128)(2,1)}), bf16[16,64,128]{2,1,0:T(8,128)(2,1)S(1)}, u32[]{:S(2)}, u32[]{:S(2)}) %all-to-all-start) | async-done | bytes 262176 | tf_op jit(solution)/shard_map/all_to_all | solution.py:345
  16.6 0.0 copy-done.4
  16.6 0.6 summary.1
  17.2 10.9 %collective-permute-start = (bf16[9,64,128]{2,1,0:T(8,128)(2,1)S(1)}, bf16[9,64,128]{2,1,0:T(8,128)(2,1)S(1)}, u32[]{:S(2)}, u32[]{:S(2)}) collective-permute-start(bf16[9,64,128]{2,1,0:T(8,128)(2,1)S(1)} %get-tuple-element.15), channel_id=1, source_target_pairs={{18,21},{9,14},{0,7},{1,6},{17,22},{8,15},{10,13},{2,5},{3,4},{27,... | collective-permute-start | bytes 442376 | tf_op jit(solution)/shard_map/ppermute | solution.py:352
  28.1 1.3 %collective-permute-start.1 = (bf16[6,64,128]{2,1,0:T(8,128)(2,1)S(1)}, bf16[6,64,128]{2,1,0:T(8,128)(2,1)S(1)}, u32[]{:S(2)}, u32[]{:S(2)}) collective-permute-start(bf16[6,64,128]{2,1,0:T(8,128)(2,1)S(1)} %get-tuple-element.16), channel_id=1, source_target_pairs={{21,18},{14,9},{7,0},{6,1},{22,17},{15,8},{13,10},{5,2},{4,3},{28,... | collective-permute-start | bytes 294920 | tf_op jit(solution)/shard_map/ppermute | solution.py:353
  29.4 10.9 %collective-permute-done.1.in_first_ref = bf16[6,64,128]{2,1,0:T(8,128)(2,1)S(1)} collective-permute-done((bf16[6,64,128]{2,1,0:T(8,128)(2,1)S(1)}, bf16[6,64,128]{2,1,0:T(8,128)(2,1)S(1)}, u32[]{:S(2)}, u32[]{:S(2)}) %collective-permute-start.1) | collective-permute-done | bytes 98336 | tf_op jit(solution)/shard_map/ppermute | solution.py:353
  40.3 0.0 collective-permute-done.in_second_ref
  40.3 0.0 copy-start.1
  40.3 0.7 paths.1
  41.0 0.0 copy-start
  41.0 0.0 copy-start.2
  41.0 0.0 copy-start.3
  41.0 22.6 %all_to_all.20 = bf16[16,192,128]{2,1,0:T(8,128)(2,1)S(1)} all-to-all(bf16[16,192,128]{2,1,0:T(8,128)(2,1)S(1)} %paths.1), channel_id=1, replica_groups={{18,9,0,1,17,8,10,2,3,27,19,11,24,16,25,26},{21,14,7,6,22,15,13,5,4,28,..., dimensions={0} | all-to-all | bytes 1572864 | tf_op jit(solution)/shard_map/all_to_all | solution.py:345
  63.6 0.0 copy-done.1
  63.6 0.0 copy-done
  63.6 0.0 copy-done.2
  63.6 0.0 copy-done.3
  63.6 9.7 %attend.1 = (bf16[128,4096]{1,0:T(8,128)(2,1)}, bf16[128,4096]{1,0:T(8,128)(2,1)}, bf16[8,2,192,128]{3,2,1,0:T(8,128)(2,1)S(1)}, f32[2,4,128,128]{3,2,1,0:T(8,128)S(1)}) custom-call(s32[32]{0:T(128)S(1)} %copy-done.4, s32[1]{0:T(128)} %bitcast.node_ref, bf16[128,4096]{1,0:T(8,128)(2,1)S(1)} %copy-done, bf16[128,4096]{1,0:T(8,128)(2,1)S(1)} %copy-done.1, ...), custom_call_target="tpu_custom_call" | custom-call | tf_op jit(solution)/shard_map/attend/pallas_call | solution.py:239
  73.3 22.5 %all_to_all.21.terms_ref = bf16[16,192,128]{2,1,0:T(8,128)(2,1)S(1)} all-to-all(bf16[16,192,128]{2,1,0:T(8,128)(2,1)S(1)} %bitcast.4), channel_id=1, replica_groups={{18,9,0,1,17,8,10,2,3,27,19,11,24,16,25,26},{21,14,7,6,22,15,13,5,4,28,..., dimensions={0} | all-to-all | bytes 1572864 | tf_op jit(solution)/shard_map/all_to_all | solution.py:345
  95.8 0.8 sum_by_owner.1
  96.6 1.3 %collective-permute-start.2 = (bf16[9,64,128]{2,1,0:T(8,128)(2,1)S(1)}, bf16[9,64,128]{2,1,0:T(8,128)(2,1)S(1)}, u32[]{:S(2)}, u32[]{:S(2)}) collective-permute-start(bf16[9,64,128]{2,1,0:T(8,128)(2,1)S(1)} %get-tuple-element.21), channel_id=1, source_target_pairs={{21,18},{14,9},{7,0},{6,1},{22,17},{15,8},{13,10},{5,2},{4,3},{28,... | collective-permute-start | bytes 442376 | tf_op jit(solution)/shard_map/ppermute | solution.py:360
  97.9 10.6 %collective-permute-start.3 = (bf16[6,64,128]{2,1,0:T(8,128)(2,1)S(1)}, bf16[6,64,128]{2,1,0:T(8,128)(2,1)S(1)}, u32[]{:S(2)}, u32[]{:S(2)}) collective-permute-start(bf16[6,64,128]{2,1,0:T(8,128)(2,1)S(1)} %get-tuple-element.22), channel_id=1, source_target_pairs={{18,21},{9,14},{0,7},{1,6},{17,22},{8,15},{10,13},{2,5},{3,4},{27,... | collective-permute-start | bytes 294920 | tf_op jit(solution)/shard_map/ppermute | solution.py:361
  108.5 1.6 %collective-permute-done.3.in_second_ref = bf16[6,64,128]{2,1,0:T(8,128)(2,1)S(1)} collective-permute-done((bf16[6,64,128]{2,1,0:T(8,128)(2,1)S(1)}, bf16[6,64,128]{2,1,0:T(8,128)(2,1)S(1)}, u32[]{:S(2)}, u32[]{:S(2)}) %collective-permute-start.3) | collective-permute-done | bytes 98336 | tf_op jit(solution)/shard_map/ppermute | solution.py:361
  110.1 0.0 collective-permute-done.2.in_first_ref
  110.2 0.7 join.1
  110.8 14.2 %all_to_all.22.below_ref = bf16[16,64,128]{2,1,0:T(8,128)(2,1)S(1)} all-to-all(bf16[16,64,128]{2,1,0:T(8,128)(2,1)S(1)} %join.1), channel_id=1, replica_groups={{18,9,0,1,17,8,10,2,3,27,19,11,24,16,25,26},{21,14,7,6,22,15,13,5,4,28,..., dimensions={0} | all-to-all | bytes 524288 | tf_op jit(solution)/shard_map/all_to_all | solution.py:345
  125.1 0.7 finish.1
Async XLA Ops:
  2.4 14.2 %all-to-all-start = ((bf16[16,64,128]{2,1,0:T(8,128)(2,1)}), bf16[16,64,128]{2,1,0:T(8,128)(2,1)S(1)}, u32[]{:S(2)}, u32[]{:S(2)}) async-start(bf16[16,64,128]{2,1,0:T(8,128)(2,1)} %cut.1), calls=%async_computation | async-start | bytes 524288 | tf_op jit(solution)/shard_map/all_to_all | solution.py:345
  12.5 4.1 %copy-start.4 = (s32[32]{0:T(128)S(1)}, s32[32]{0:T(128)}, u32[]{:S(2)}) copy-start(s32[32]{0:T(128)} %depth_ref.9) | copy-start | bytes 388
  17.2 23.1 %collective-permute-start = (bf16[9,64,128]{2,1,0:T(8,128)(2,1)S(1)}, bf16[9,64,128]{2,1,0:T(8,128)(2,1)S(1)}, u32[]{:S(2)}, u32[]{:S(2)}) collective-permute-start(bf16[9,64,128]{2,1,0:T(8,128)(2,1)S(1)} %get-tuple-element.15), channel_id=1, source_target_pairs={{18,21},{9,14},{0,7},{1,6},{17,22},{8,15},{10,13},{2,5},{3,4},{27,... | collective-permute-start | bytes 442376 | tf_op jit(solution)/shard_map/ppermute | solution.py:352
  28.1 12.2 %collective-permute-start.1 = (bf16[6,64,128]{2,1,0:T(8,128)(2,1)S(1)}, bf16[6,64,128]{2,1,0:T(8,128)(2,1)S(1)}, u32[]{:S(2)}, u32[]{:S(2)}) collective-permute-start(bf16[6,64,128]{2,1,0:T(8,128)(2,1)S(1)} %get-tuple-element.16), channel_id=1, source_target_pairs={{21,18},{14,9},{7,0},{6,1},{22,17},{15,8},{13,10},{5,2},{4,3},{28,... | collective-permute-start | bytes 294920 | tf_op jit(solution)/shard_map/ppermute | solution.py:353
  40.3 23.3 %copy-start.1 = (bf16[128,4096]{1,0:T(8,128)(2,1)S(1)}, bf16[128,4096]{1,0:T(8,128)(2,1)}, u32[]{:S(2)}) copy-start(bf16[128,4096]{1,0:T(8,128)(2,1)} %do_ref.1) | copy-start | bytes 3145732
  41.0 22.6 %copy-start = (bf16[128,4096]{1,0:T(8,128)(2,1)S(1)}, bf16[128,4096]{1,0:T(8,128)(2,1)}, u32[]{:S(2)}) copy-start(bf16[128,4096]{1,0:T(8,128)(2,1)} %q_ref.1) | copy-start | bytes 3145732
  41.0 22.6 %copy-start.2 = (bf16[128,512]{1,0:T(8,128)(2,1)S(1)}, bf16[128,512]{1,0:T(8,128)(2,1)}, u32[]{:S(2)}) copy-start(bf16[128,512]{1,0:T(8,128)(2,1)} %k_ref.3) | copy-start | bytes 393220
  41.0 22.6 %copy-start.3 = (bf16[128,512]{1,0:T(8,128)(2,1)S(1)}, bf16[128,512]{1,0:T(8,128)(2,1)}, u32[]{:S(2)}) copy-start(bf16[128,512]{1,0:T(8,128)(2,1)} %v_ref.3) | copy-start | bytes 393220
  96.6 13.5 %collective-permute-start.2 = (bf16[9,64,128]{2,1,0:T(8,128)(2,1)S(1)}, bf16[9,64,128]{2,1,0:T(8,128)(2,1)S(1)}, u32[]{:S(2)}, u32[]{:S(2)}) collective-permute-start(bf16[9,64,128]{2,1,0:T(8,128)(2,1)S(1)} %get-tuple-element.21), channel_id=1, source_target_pairs={{21,18},{14,9},{7,0},{6,1},{22,17},{15,8},{13,10},{5,2},{4,3},{28,... | collective-permute-start | bytes 442376 | tf_op jit(solution)/shard_map/ppermute | solution.py:360
  97.9 12.2 %collective-permute-start.3 = (bf16[6,64,128]{2,1,0:T(8,128)(2,1)S(1)}, bf16[6,64,128]{2,1,0:T(8,128)(2,1)S(1)}, u32[]{:S(2)}, u32[]{:S(2)}) collective-permute-start(bf16[6,64,128]{2,1,0:T(8,128)(2,1)S(1)} %get-tuple-element.22), channel_id=1, source_target_pairs={{18,21},{9,14},{0,7},{1,6},{17,22},{8,15},{10,13},{2,5},{3,4},{27,... | collective-permute-start | bytes 294920 | tf_op jit(solution)/shard_map/ppermute | solution.py:361

commit v6 on v5

--- a/solution.py
+++ b/solution.py
@@ -24,13 +24,14 @@
 NEG = -1e30
 F32 = jnp.float32
 BF16 = jnp.bfloat16
+PARTNER = (7, 5, 6, 4)
 ORDER = (
     (2, 2), (1, 1), (0, 0), (0, 1), (2, 1), (1, 0), (1, 2), (0, 2),
     (0, 3), (3, 3), (2, 3), (1, 3), (3, 0), (2, 0), (3, 1), (3, 2),
 )
 HALVES = [
     [y * COLS + q for y, q in ORDER],
-    [y * COLS + COLS - 1 - q for y, q in ORDER],
+    [y * COLS + PARTNER[q] for y, q in ORDER],
 ]
 MEMBER = {node: member for half in HALVES for member, node in enumerate(half)}
 TO_SECOND = list(zip(HALVES[0], HALVES[1]))

time: 128 us -> 128 us (level)
  no operation moved by 1% of the time
where the time goes in v6:
time: 128 us; the launch traced here: 126 us
  blocking collectives  58.9 us (46%)
  starting transfers between devices  34.5 us (27%)
  waiting for transfers between devices  16.5 us (13%)
  Pallas kernels  14.9 us (12%)
    all_to_all x3, blocking collectives, exchange(): return lax.all_to_all(array, 'node', 0, 0, axis_index_groups=HALVES)  58.9 us
    ppermute x2, starting transfers between devices, local(): in_second = lax.ppermute(for_second, 'node', TO_SECOND)  21.8 us
    ppermute x2, waiting for transfers between devices, local(): in_first = lax.ppermute(for_first, 'node', TO_FIRST)  10.8 us
    all_to_all x1, starting transfers between devices, exchange(): return lax.all_to_all(array, 'node', 0, 0, axis_index_groups=HALVES)  10.1 us
    pallas_call x1, Pallas kernels, attend(): pl.pallas_call(main_kernel, out_shape=(jax.ShapeDtypeStruct(queries.shape...  9.66 us
    all_to_all x1, waiting for transfers between devices, exchange(): return lax.all_to_all(array, 'node', 0, 0, axis_index_groups=HALVES)  4.08 us
    ppermute x2, starting transfers between devices, local(): in_first = lax.ppermute(for_first, 'node', TO_FIRST)  2.58 us
  transfers between devices with their start and end apart: 5, of which 3 were waited for; matrix products, arithmetic and copies ran while one was open for 0% of the time, Pallas kernels for 0%

profile of v6, /device:TPU:1, one launch (start us, length us, event | category | flops | bytes accessed | tf_op | source)
XLA Modules:
  0.0 125.5 jit_solution(17503636096250400005)
XLA Ops:
  0.6 1.7 %cut.1 = bf16[16,64,128]{2,1,0:T(8,128)(2,1)} custom-call(bf16[128,512]{1,0:T(8,128)(2,1)} %k_ref.3, bf16[128,512]{1,0:T(8,128)(2,1)} %v_ref.3), custom_call_target="tpu_custom_call" | custom-call | tf_op jit(solution)/shard_map/cut/pallas_call | solution.py:100
  2.4 10.1 %all-to-all-start = ((bf16[16,64,128]{2,1,0:T(8,128)(2,1)}), bf16[16,64,128]{2,1,0:T(8,128)(2,1)S(1)}, u32[]{:S(2)}, u32[]{:S(2)}) async-start(bf16[16,64,128]{2,1,0:T(8,128)(2,1)} %cut.1), calls=%async_computation | async-start | bytes 524288 | tf_op jit(solution)/shard_map/all_to_all | solution.py:346
  12.5 0.0 copy-start.4
  12.5 4.1 %all-to-all-done.held_ref = bf16[16,64,128]{2,1,0:T(8,128)(2,1)S(1)} async-done(((bf16[16,64,128]{2,1,0:T(8,128)(2,1)}), bf16[16,64,128]{2,1,0:T(8,128)(2,1)S(1)}, u32[]{:S(2)}, u32[]{:S(2)}) %all-to-all-start) | async-done | bytes 262176 | tf_op jit(solution)/shard_map/all_to_all | solution.py:346
  16.6 0.0 copy-done.4
  16.6 0.6 summary.1
  17.2 11.2 %collective-permute-start = (bf16[9,64,128]{2,1,0:T(8,128)(2,1)S(1)}, bf16[9,64,128]{2,1,0:T(8,128)(2,1)S(1)}, u32[]{:S(2)}, u32[]{:S(2)}) collective-permute-start(bf16[9,64,128]{2,1,0:T(8,128)(2,1)S(1)} %get-tuple-element.15), channel_id=1, source_target_pairs={{18,22},{9,13},{0,7},{1,5},{17,21},{8,15},{10,14},{2,6},{3,4},{27,... | collective-permute-start | bytes 442376 | tf_op jit(solution)/shard_map/ppermute | solution.py:353
  28.4 1.3 %collective-permute-start.1 = (bf16[6,64,128]{2,1,0:T(8,128)(2,1)S(1)}, bf16[6,64,128]{2,1,0:T(8,128)(2,1)S(1)}, u32[]{:S(2)}, u32[]{:S(2)}) collective-permute-start(bf16[6,64,128]{2,1,0:T(8,128)(2,1)S(1)} %get-tuple-element.16), channel_id=1, source_target_pairs={{22,18},{13,9},{7,0},{5,1},{21,17},{15,8},{14,10},{6,2},{4,3},{28,... | collective-permute-start | bytes 294920 | tf_op jit(solution)/shard_map/ppermute | solution.py:354
  29.7 10.8 %collective-permute-done.1.in_first_ref = bf16[6,64,128]{2,1,0:T(8,128)(2,1)S(1)} collective-permute-done((bf16[6,64,128]{2,1,0:T(8,128)(2,1)S(1)}, bf16[6,64,128]{2,1,0:T(8,128)(2,1)S(1)}, u32[]{:S(2)}, u32[]{:S(2)}) %collective-permute-start.1) | collective-permute-done | bytes 98336 | tf_op jit(solution)/shard_map/ppermute | solution.py:354
  40.5 0.0 collective-permute-done.in_second_ref
  40.5 0.0 copy-start.1
  40.5 0.7 paths.1
  41.2 0.0 copy-start
  41.2 0.0 copy-start.2
  41.2 0.0 copy-start.3
  41.2 22.4 %all_to_all.20 = bf16[16,192,128]{2,1,0:T(8,128)(2,1)S(1)} all-to-all(bf16[16,192,128]{2,1,0:T(8,128)(2,1)S(1)} %paths.1), channel_id=1, replica_groups={{18,9,0,1,17,8,10,2,3,27,19,11,24,16,25,26},{22,13,7,5,21,15,14,6,4,28,..., dimensions={0} | all-to-all | bytes 1572864 | tf_op jit(solution)/shard_map/all_to_all | solution.py:346
  63.6 0.0 copy-done.1
  63.6 0.0 copy-done
  63.6 0.0 copy-done.2
  63.6 0.0 copy-done.3
  63.6 9.7 %attend.1 = (bf16[128,4096]{1,0:T(8,128)(2,1)}, bf16[128,4096]{1,0:T(8,128)(2,1)}, bf16[8,2,192,128]{3,2,1,0:T(8,128)(2,1)S(1)}, f32[2,4,128,128]{3,2,1,0:T(8,128)S(1)}) custom-call(s32[32]{0:T(128)S(1)} %copy-done.4, s32[1]{0:T(128)} %bitcast.node_ref, bf16[128,4096]{1,0:T(8,128)(2,1)S(1)} %copy-done, bf16[128,4096]{1,0:T(8,128)(2,1)S(1)} %copy-done.1, ...), custom_call_target="tpu_custom_call" | custom-call | tf_op jit(solution)/shard_map/attend/pallas_call | solution.py:240
  73.3 22.6 %all_to_all.21.terms_ref = bf16[16,192,128]{2,1,0:T(8,128)(2,1)S(1)} all-to-all(bf16[16,192,128]{2,1,0:T(8,128)(2,1)S(1)} %bitcast.4), channel_id=1, replica_groups={{18,9,0,1,17,8,10,2,3,27,19,11,24,16,25,26},{22,13,7,5,21,15,14,6,4,28,..., dimensions={0} | all-to-all | bytes 1572864 | tf_op jit(solution)/shard_map/all_to_all | solution.py:346
  95.9 0.8 sum_by_owner.1
  96.7 1.3 %collective-permute-start.2 = (bf16[9,64,128]{2,1,0:T(8,128)(2,1)S(1)}, bf16[9,64,128]{2,1,0:T(8,128)(2,1)S(1)}, u32[]{:S(2)}, u32[]{:S(2)}) collective-permute-start(bf16[9,64,128]{2,1,0:T(8,128)(2,1)S(1)} %get-tuple-element.21), channel_id=1, source_target_pairs={{22,18},{13,9},{7,0},{5,1},{21,17},{15,8},{14,10},{6,2},{4,3},{28,... | collective-permute-start | bytes 442376 | tf_op jit(solution)/shard_map/ppermute | solution.py:361
  98.0 10.6 %collective-permute-start.3 = (bf16[6,64,128]{2,1,0:T(8,128)(2,1)S(1)}, bf16[6,64,128]{2,1,0:T(8,128)(2,1)S(1)}, u32[]{:S(2)}, u32[]{:S(2)}) collective-permute-start(bf16[6,64,128]{2,1,0:T(8,128)(2,1)S(1)} %get-tuple-element.22), channel_id=1, source_target_pairs={{18,22},{9,13},{0,7},{1,5},{17,21},{8,15},{10,14},{2,6},{3,4},{27,... | collective-permute-start | bytes 294920 | tf_op jit(solution)/shard_map/ppermute | solution.py:362
  108.6 1.6 %collective-permute-done.3.in_second_ref = bf16[6,64,128]{2,1,0:T(8,128)(2,1)S(1)} collective-permute-done((bf16[6,64,128]{2,1,0:T(8,128)(2,1)S(1)}, bf16[6,64,128]{2,1,0:T(8,128)(2,1)S(1)}, u32[]{:S(2)}, u32[]{:S(2)}) %collective-permute-start.3) | collective-permute-done | bytes 98336 | tf_op jit(solution)/shard_map/ppermute | solution.py:362
  110.2 0.0 collective-permute-done.2.in_first_ref
  110.2 0.7 join.1
  110.9 13.9 %all_to_all.22.below_ref = bf16[16,64,128]{2,1,0:T(8,128)(2,1)S(1)} all-to-all(bf16[16,64,128]{2,1,0:T(8,128)(2,1)S(1)} %join.1), channel_id=1, replica_groups={{18,9,0,1,17,8,10,2,3,27,19,11,24,16,25,26},{22,13,7,5,21,15,14,6,4,28,..., dimensions={0} | all-to-all | bytes 524288 | tf_op jit(solution)/shard_map/all_to_all | solution.py:346
  124.8 0.7 finish.1
Async XLA Ops:
  2.4 14.2 %all-to-all-start = ((bf16[16,64,128]{2,1,0:T(8,128)(2,1)}), bf16[16,64,128]{2,1,0:T(8,128)(2,1)S(1)}, u32[]{:S(2)}, u32[]{:S(2)}) async-start(bf16[16,64,128]{2,1,0:T(8,128)(2,1)} %cut.1), calls=%async_computation | async-start | bytes 524288 | tf_op jit(solution)/shard_map/all_to_all | solution.py:346
  12.5 4.1 %copy-start.4 = (s32[32]{0:T(128)S(1)}, s32[32]{0:T(128)}, u32[]{:S(2)}) copy-start(s32[32]{0:T(128)} %depth_ref.9) | copy-start | bytes 388
  17.2 23.3 %collective-permute-start = (bf16[9,64,128]{2,1,0:T(8,128)(2,1)S(1)}, bf16[9,64,128]{2,1,0:T(8,128)(2,1)S(1)}, u32[]{:S(2)}, u32[]{:S(2)}) collective-permute-start(bf16[9,64,128]{2,1,0:T(8,128)(2,1)S(1)} %get-tuple-element.15), channel_id=1, source_target_pairs={{18,22},{9,13},{0,7},{1,5},{17,21},{8,15},{10,14},{2,6},{3,4},{27,... | collective-permute-start | bytes 442376 | tf_op jit(solution)/shard_map/ppermute | solution.py:353
  28.4 12.1 %collective-permute-start.1 = (bf16[6,64,128]{2,1,0:T(8,128)(2,1)S(1)}, bf16[6,64,128]{2,1,0:T(8,128)(2,1)S(1)}, u32[]{:S(2)}, u32[]{:S(2)}) collective-permute-start(bf16[6,64,128]{2,1,0:T(8,128)(2,1)S(1)} %get-tuple-element.16), channel_id=1, source_target_pairs={{22,18},{13,9},{7,0},{5,1},{21,17},{15,8},{14,10},{6,2},{4,3},{28,... | collective-permute-start | bytes 294920 | tf_op jit(solution)/shard_map/ppermute | solution.py:354
  40.5 23.1 %copy-start.1 = (bf16[128,4096]{1,0:T(8,128)(2,1)S(1)}, bf16[128,4096]{1,0:T(8,128)(2,1)}, u32[]{:S(2)}) copy-start(bf16[128,4096]{1,0:T(8,128)(2,1)} %do_ref.1) | copy-start | bytes 3145732
  41.2 22.4 %copy-start = (bf16[128,4096]{1,0:T(8,128)(2,1)S(1)}, bf16[128,4096]{1,0:T(8,128)(2,1)}, u32[]{:S(2)}) copy-start(bf16[128,4096]{1,0:T(8,128)(2,1)} %q_ref.1) | copy-start | bytes 3145732
  41.2 22.4 %copy-start.2 = (bf16[128,512]{1,0:T(8,128)(2,1)S(1)}, bf16[128,512]{1,0:T(8,128)(2,1)}, u32[]{:S(2)}) copy-start(bf16[128,512]{1,0:T(8,128)(2,1)} %k_ref.3) | copy-start | bytes 393220
  41.2 22.4 %copy-start.3 = (bf16[128,512]{1,0:T(8,128)(2,1)S(1)}, bf16[128,512]{1,0:T(8,128)(2,1)}, u32[]{:S(2)}) copy-start(bf16[128,512]{1,0:T(8,128)(2,1)} %v_ref.3) | copy-start | bytes 393220
  96.7 13.5 %collective-permute-start.2 = (bf16[9,64,128]{2,1,0:T(8,128)(2,1)S(1)}, bf16[9,64,128]{2,1,0:T(8,128)(2,1)S(1)}, u32[]{:S(2)}, u32[]{:S(2)}) collective-permute-start(bf16[9,64,128]{2,1,0:T(8,128)(2,1)S(1)} %get-tuple-element.21), channel_id=1, source_target_pairs={{22,18},{13,9},{7,0},{5,1},{21,17},{15,8},{14,10},{6,2},{4,3},{28,... | collective-permute-start | bytes 442376 | tf_op jit(solution)/shard_map/ppermute | solution.py:361
  98.0 12.2 %collective-permute-start.3 = (bf16[6,64,128]{2,1,0:T(8,128)(2,1)S(1)}, bf16[6,64,128]{2,1,0:T(8,128)(2,1)S(1)}, u32[]{:S(2)}, u32[]{:S(2)}) collective-permute-start(bf16[6,64,128]{2,1,0:T(8,128)(2,1)S(1)} %get-tuple-element.22), channel_id=1, source_target_pairs={{18,22},{9,13},{0,7},{1,5},{17,21},{8,15},{10,14},{2,6},{3,4},{27,... | collective-permute-start | bytes 294920 | tf_op jit(solution)/shard_map/ppermute | solution.py:362
